TPU v7x, 32 devices: a whole 2x2x4 slice. The times are simulated.
32 devices in a mesh: tm: 4 (over y, core), chan: 8 (over z, x).
Axes of the slice: x: 2, y: 2, z: 4, core: 2. Of those that a mesh axis runs over, the one named last changes fastest.
Arguments:
- strain: float32 [256, 16384], P('chan', 'tm'), may hold values from -16 to 16
- channel_mask: int32 [256], P('chan'), may hold values 0 or 1
Outputs:
- cleaned: float32 [256, 16384], P('chan', 'tm')
All inputs are finite; a program needn't handle non-finite values. No bound on the sum of `channel_mask` on one device may be relied on, other than what follows from the above.
Results may differ from a plain program's by a relative error of at most 0.0003.
Values sent between devices are 32-bit elements; how exact they have to be, the bound alone decides.
No kernel may reach another device: no remote copies, remote signals or barrier semaphores. Data moves between devices by JAX's collectives and lax.ppermute only.
A program may use at most 64 MiB of HBM per device.

v0:
```python
import math

import jax
import jax.numpy as jnp
import numpy as np
from jax import lax
from jax.sharding import PartitionSpec as P

RADIUS = 16


low_corner = 0.015
high_corner = 100.0
sample_rate = 500.0
highest = lax.Precision.HIGHEST


def carried_in(value, axis, combine, identity, reverse):
    size, index = (lax.axis_size(axis), lax.axis_index(axis))
    everything = jax.tree.map(lambda part: lax.all_gather(part, axis), value)
    start = jax.tree.map(
        lambda part, zero: jnp.broadcast_to(jnp.asarray(zero, part.dtype), part.shape),
        value,
        identity,
    )

    def lap(k, before):
        at = size - 1 - k if reverse else k
        reached = at > index if reverse else at < index
        new = combine(before, jax.tree.map(lambda part: part[at], everything))
        return jax.tree.map(lambda a, b: jnp.where(reached, a, b), new, before)

    return lax.fori_loop(0, size, lap, start)


def with_halo(value, sides, width):
    for axis, dim in sides:
        size, length = (lax.axis_size(axis), value.shape[dim])
        up = [(i, (i + 1) % size) for i in range(size - 1)]
        down = [(j, i) for i, j in up]
        last = lax.slice_in_dim(value, length - width, length, axis=dim)
        leading = lax.slice_in_dim(value, 0, width, axis=dim)
        before = lax.ppermute(last, axis, up)
        after = lax.ppermute(leading, axis, down)
        value = jnp.concatenate([before, value, after], axis=dim)
    return value


def section(corner, highpass):
    warped = 2.0 * sample_rate * math.tan(math.pi * corner / sample_rate)
    scaled = warped / (2.0 * sample_rate * math.sqrt(2.0))
    numer_real = 1.0 - scaled
    denom_real = 1.0 + scaled
    denom_imag = -scaled
    modulus = denom_real * denom_real + denom_imag * denom_imag
    pole_real = (numer_real * denom_real + scaled * denom_imag) / modulus
    pole_imag = (scaled * denom_real - numer_real * denom_imag) / modulus
    pole_norm = pole_real * pole_real + pole_imag * pole_imag
    zero_place = 1.0 if highpass else -1.0
    section_gain = ((1.0 + zero_place * pole_real) ** 2 + pole_imag * pole_imag) / 4.0
    linear = section_gain * (2.0 * pole_real - 2.0 * zero_place)
    constant = section_gain * (1.0 - pole_norm)
    shrink = 1.0 - math.sqrt(pole_norm)
    first_out = linear / shrink
    second = (constant + pole_real * linear) / (pole_imag * shrink)
    rotation = np.array([[pole_real, -pole_imag], [pole_imag, pole_real]])
    inject = np.array([shrink, 0.0])
    return (rotation, inject, np.array([first_out, second]), section_gain)


def filter_system():
    high_rotation, high_inject, high_out, high_gain = section(low_corner, True)
    low_rotation, low_inject, low_out, low_gain = section(high_corner, False)
    upper_rows = np.concatenate([high_rotation, np.zeros((2, 2))], axis=1)
    lower_rows = np.concatenate([np.outer(low_inject, high_out), low_rotation], axis=1)
    transition = np.concatenate([upper_rows, lower_rows], axis=0)
    driving = np.concatenate([high_inject, low_inject * high_gain])
    readout = np.concatenate([high_out * low_gain, low_out])
    direct = low_gain * high_gain
    return (transition, driving, readout, direct)


def spatial_taps(extent):
    positions = np.arange(-extent, extent + 1)
    window = 0.5 * (1.0 + np.cos(np.pi * positions / (extent + 1)))
    window = window / np.sum(window)
    return np.where(positions == 0, 1.0 - window, -window)


def filter_tables(block_size, number_blocks):
    transition, driving, readout, direct = filter_system()
    step_powers = [np.eye(4)]
    for counter in range(block_size):
        step_powers.append(step_powers[-1] @ transition)
    response = np.array(
        [direct] + [readout @ step_powers[counter] @ driving for counter in range(block_size - 1)]
    )
    lag_table = np.arange(block_size)[None, :] - np.arange(block_size)[:, None]
    toeplitz = np.where(lag_table >= 0, response[np.clip(lag_table, 0, block_size - 1)], 0.0)
    inputs_to_end = np.stack(
        [step_powers[block_size - 1 - counter] @ driving for counter in range(block_size)], axis=1
    )
    state_to_output = np.stack(
        [readout @ step_powers[counter] for counter in range(block_size)], axis=1
    )
    levels = [np.eye(4)]
    for counter in range(number_blocks):
        levels.append(levels[-1] @ step_powers[block_size])
    levels = np.stack(levels)
    distance = np.arange(number_blocks)[:, None] - np.arange(number_blocks)[None, :] - 1
    chain_powers = np.where(
        (distance >= 0)[:, :, None, None], levels[np.clip(distance, 0, number_blocks)], 0.0
    )
    carry_in = levels[:number_blocks]
    tail_powers = levels[np.arange(number_blocks - 1, -1, -1)]
    device_power = levels[number_blocks]
    return tuple(
        (
            jnp.asarray(table, jnp.float32)
            for table in (
                toeplitz,
                inputs_to_end,
                state_to_output,
                chain_powers,
                carry_in,
                tail_powers,
                device_power,
            )
        )
    )


def boundary(device_power, device_end, reverse):

    def combine(earlier, later):
        return (
            jnp.dot(later[0], earlier[0], precision=highest),
            jnp.dot(later[0], earlier[1], precision=highest) + later[1],
        )

    identity = (jnp.eye(4, dtype=jnp.float32), jnp.zeros_like(device_end))
    composed = carried_in((device_power, device_end), "tm", combine, identity, reverse)
    return composed[1]


def local_pass(record, tables, reverse):
    channels, samples = record.shape
    toeplitz, inputs_to_end, state_to_output, chain_powers, carry_in, tail_powers, device_power = (
        tables
    )
    blocks = record.reshape(channels, samples // 128, 128)
    unforced = jnp.einsum("cbm,mk->cbk", blocks, toeplitz, precision=highest)
    block_ends = jnp.einsum("pm,cbm->pcb", inputs_to_end, blocks, precision=highest)
    starts = jnp.einsum("bjpq,qcj->pcb", chain_powers, block_ends, precision=highest)
    device_end = jnp.einsum("jpq,qcj->pc", tail_powers, block_ends, precision=highest)
    entering = boundary(device_power, device_end, reverse)
    starts = starts + jnp.einsum("bpq,qc->pcb", carry_in, entering, precision=highest)
    result = unforced + jnp.einsum("pk,pcb->cbk", state_to_output, starts, precision=highest)
    return result.reshape(channels, samples)


def bandpass(record, tables):
    forward = local_pass(record, tables, False)
    backward = local_pass(jnp.flip(forward, axis=1), tables, True)
    return jnp.flip(backward, axis=1)


def shards(strain, channel_mask):
    channels, samples = strain.shape
    tables = filter_tables(128, samples // 128)
    weighting = channel_mask.astype(jnp.float32)[:, None]
    taps = spatial_taps(RADIUS)
    lag_table = np.arange(channels + 2 * RADIUS)[None, :] - np.arange(channels)[:, None]
    band_matrix = np.where(
        (lag_table >= 0) & (lag_table <= 2 * RADIUS), taps[np.clip(lag_table, 0, 2 * RADIUS)], 0.0
    )
    band_matrix = jnp.asarray(band_matrix, jnp.float32)
    filtered = bandpass(strain, tables) * weighting
    padded = with_halo(filtered, (("chan", 0),), RADIUS)
    return jnp.dot(band_matrix, padded, precision=highest)


def solution(mesh):
    placed = (P("chan", "tm"), P("chan"))
    return jax.shard_map(
        shards, mesh=mesh, in_specs=placed, out_specs=P("chan", "tm"), check_vma=False
    )
```

profile of v0, /device:TPU:0, one launch (start us, length us, event | category | flops | bytes accessed | tf_op | source)
XLA Modules:
  0.0 53.5 jit_solution(222061023492357658)
XLA Ops:
  0.0 0.7 %copy-done.9 = f32[1,4,4]{2,1,0:T(4,128)S(1)} copy-done((f32[1,4,4]{2,1,0:T(4,128)S(1)}, f32[1,4,4]{2,1,0:T(4,128)}, u32[]{:S(2)}) %copy-start.9) | copy-done | bytes 88
  0.7 6.1 %all_gather.21 = f32[4,4,4]{2,1,0:T(4,128)S(1)} all-gather(f32[1,4,4]{2,1,0:T(4,128)S(1)} %copy-done.9), channel_id=1, replica_groups=mesh['tm'=4,'chan'=8] {'tm'}, dimensions={0}, use_global_device_ids=true | all-gather | bytes 320 | tf_op jit(solution)/shard_map/all_gather | solution.py:20
  6.8 1.1 %copy.23 = f32[4,8,32,128]{3,2,1,0:T(8,128)S(1)} copy(f32[4,8,32,128]{3,1,2,0:T(8,128)} %bitcast.96) | data formatting | bytes 1048576
  8.0 2.1 %fusion.31 = f32[4,32,32]{2,0,1:T(4,128)S(1)} fusion(f32[4,128,1]{1,0,2:T(4,128)S(1)} %copy-done.8, f32[32,32,128]{2,1,0:T(8,128)S(1)} %bitcast.89), kind=kOutput, calls=%fused_computation.46 | convolution fusion | flops 6291456 | bytes 542720 | tf_op jit(solution)/shard_map/pm,cbm->pcb/dot_general | solution.py:153
  10.1 0.6 %convolution_bitcast_fusion = f32[32,32,128]{2,1,0:T(8,128)S(1)} fusion(f32[128,128,1]{1,0,2:T(8,128)S(1)} %copy-done.1, f32[32,32,128]{2,1,0:T(8,128)S(1)} %bitcast.90), kind=kOutput, calls=%fused_computation.23 | convolution fusion | flops 201326592 | bytes 1114112 | tf_op jit(solution)/shard_map/cbm,mk->cbk/dot_general | solution.py:152
  11.1 0.7 %convolution_bitcast_fusion.2 = f32[32,32,4]{1,0,2:T(8,128)S(1)} fusion(f32[32,32,4,4]{1,0,3,2:T(8,128)S(1)} %copy-done, f32[4,32,32]{2,0,1:T(4,128)S(1)} %fusion.31), kind=kOutput, calls=%fused_computation.29 | convolution fusion | flops 6291456 | bytes 98304 | tf_op jit(solution)/shard_map/bjpq,qcj->pcb/dot_general | solution.py:154
  11.8 5.4 %all-gather.2 = f32[4,4,32]{2,1,0:T(4,128)S(1)} all-gather(f32[1,4,32]{2,1,0:T(4,128)S(1)} %convolution_bitcast_fusion.4), channel_id=2, replica_groups=mesh['tm'=4,'chan'=8] {'tm'}, dimensions={0}, use_global_device_ids=true | all-gather | bytes 2560 | tf_op jit(solution)/shard_map/all_gather | solution.py:20
  17.2 0.6 %while.30 = (s32[]{:T(128)}, f32[4,32]{1,0:T(4,128)S(1)}, s32[]{:T(128)}, f32[4,4,4]{2,1,0:T(4,128)S(1)}, f32[4,4,32]{2,1,0:T(4,128)S(1)}, /*index=5*/s32[]{:T(128)}, s32[]{:T(128)}) while((s32[]{:T(128)}, f32[4,32]{1,0:T(4,128)S(1)}, s32[]{:T(128)}, f32[4,4,4]{2,1,0:T(4,128)S(1)}, f32[4,4,32]{2,1,0:T(4,128)S(1)}, ...), condition=%wide.region_1.2_spmd.clone, body=%wide.region_0.1_spmd.clone.sunk | while | flops 6660 | bytes 12391 | solution.py:33
  18.6 1.0 %convolution_add_fusion.4 = f32[32,32,128]{2,1,0:T(8,128)S(1)} fusion(f32[32,32,128]{2,1,0:T(8,128)S(1)} %convolution_bitcast_fusion, f32[4,128,1]{1,0,2:T(4,128)S(1)} %copy-done.7, f32[4,32,32]{2,1,0:T(8,128)S(1)} %fusion.19), kind=kOutput, calls=%fused_computation.22 | convolution fusion | flops 6422528 | bytes 1067008 | tf_op jit(solution)/shard_map/pk,pcb->cbk/dot_general | solution.py:158
  19.9 2.3 %rev.7 = f32[32,4096]{1,0:T(8,128)S(1)} reverse(f32[32,4096]{1,0:T(8,128)S(1)} %bitcast.93), dimensions={1} | reverse | bytes 1048576 | tf_op jit(solution)/shard_map/jit(_flip)/rev | solution.py:164
  22.4 2.1 %fusion.33 = f32[4,32,32]{2,0,1:T(4,128)S(1)} fusion(f32[4,128,1]{1,0,2:T(4,128)S(1)} %copy-done.8, f32[32,32,128]{2,1,0:T(8,128)S(1)} %bitcast.87), kind=kOutput, calls=%fused_computation.48 | convolution fusion | flops 6291456 | bytes 542720 | tf_op jit(solution)/shard_map/pm,cbm->pcb/dot_general | solution.py:153
  24.5 0.6 %fusion.32 = f32[32,32,128]{2,1,0:T(8,128)S(1)} fusion(f32[32,32,128]{2,1,0:T(8,128)S(1)} %bitcast.88, f32[128,128,1]{1,0,2:T(8,128)S(1)} %copy-done.1), kind=kOutput, calls=%fused_computation.47 | convolution fusion | flops 201326592 | bytes 1114112 | tf_op jit(solution)/shard_map/cbm,mk->cbk/dot_general | solution.py:152
  25.3 0.7 %convolution_bitcast_fusion.1 = f32[32,32,4]{1,0,2:T(8,128)S(1)} fusion(f32[32,32,4,4]{1,0,3,2:T(8,128)S(1)} %copy-done, f32[4,32,32]{2,0,1:T(4,128)S(1)} %fusion.33), kind=kOutput, calls=%fused_computation.26 | convolution fusion | flops 6291456 | bytes 98304 | tf_op jit(solution)/shard_map/bjpq,qcj->pcb/dot_general | solution.py:154
  26.0 5.2 %all-gather.3 = f32[4,4,32]{2,1,0:T(4,128)S(1)} all-gather(f32[1,4,32]{2,1,0:T(4,128)S(1)} %convolution_bitcast_fusion.3), channel_id=3, replica_groups=mesh['tm'=4,'chan'=8] {'tm'}, dimensions={0}, use_global_device_ids=true | all-gather | bytes 2560 | tf_op jit(solution)/shard_map/all_gather | solution.py:20
  31.2 0.6 %while.31 = (s32[]{:T(128)}, f32[4,32]{1,0:T(4,128)S(1)}, s32[]{:T(128)}, f32[4,4,4]{2,1,0:T(4,128)S(1)}, f32[4,4,32]{2,1,0:T(4,128)S(1)}, /*index=5*/s32[]{:T(128)}, s32[]{:T(128)}, s32[]{:T(128)}, s32[]{:T(128)}) while((s32[]{:T(128)}, f32[4,32]{1,0:T(4,128)S(1)}, s32[]{:T(128)}, f32[4,4,4]{2,1,0:T(4,128)S(1)}, ...), condition=%wide.region_3.4_spmd.clone, body=%wide.region_2.3_spmd.clone.sunk | while | flops 6664 | bytes 12453 | solution.py:33
  32.1 1.0 %convolution_add_fusion.3 = f32[32,32,128]{2,1,0:T(8,128)S(1)} fusion(f32[32,32,128]{2,1,0:T(8,128)S(1)} %fusion.32, f32[4,128,1]{1,0,2:T(4,128)S(1)} %copy-done.7, f32[4,32,32]{2,1,0:T(8,128)S(1)} %fusion.18), kind=kOutput, calls=%fused_computation.21 | convolution fusion | flops 6422528 | bytes 1067008 | tf_op jit(solution)/shard_map/pk,pcb->cbk/dot_general | solution.py:158
  33.4 2.3 %rev.8 = f32[32,4096]{1,0:T(8,128)S(1)} reverse(f32[32,4096]{1,0:T(8,128)S(1)} %bitcast.95), dimensions={1} | reverse | bytes 1048576 | tf_op jit(solution)/shard_map/jit(_flip)/rev | solution.py:165
  36.0 1.3 %collective-permute-start.1 = (f32[16,4096]{1,0:T(8,128)S(1)}, f32[16,4096]{1,0:T(8,128)S(1)}, u32[]{:S(2)}, u32[]{:S(2)}) collective-permute-start(f32[16,4096]{1,0:T(8,128)S(1)} %get-tuple-element.290), channel_id=1, source_target_pairs={{1,0},{2,1},{3,2},{4,3},{5,4},{6,5},{7,6},{9,8},{10,9},{11,10},{12... | collective-permute-start | bytes 786440 | tf_op jit(solution)/shard_map/ppermute | solution.py:44
  37.3 4.6 %collective-permute-start = (f32[16,4096]{1,0:T(8,128)S(1)}, f32[16,4096]{1,0:T(8,128)S(1)}, u32[]{:S(2)}, u32[]{:S(2)}) collective-permute-start(f32[16,4096]{1,0:T(8,128)S(1)} %get-tuple-element.289), channel_id=1, source_target_pairs={{0,1},{1,2},{2,3},{3,4},{4,5},{5,6},{6,7},{8,9},{9,10},{10,11},{11... | collective-permute-start | bytes 786440 | tf_op jit(solution)/shard_map/ppermute | solution.py:43
  41.9 0.6 %fusion.34 = f32[4096,32]{0,1:T(8,128)S(1)} fusion(f32[32,4096]{1,0:T(8,128)S(1)} %broadcast_multiply_fusion, f32[32,32]{1,0:T(8,128)S(1)} %copy-done.5), kind=kOutput, calls=%fused_computation.49 | convolution fusion | flops 50331648 | bytes 1052672 | tf_op jit(solution)/shard_map/dot_general | solution.py:180
  42.4 3.9 %collective-permute-done.1 = f32[16,4096]{1,0:T(8,128)S(1)} collective-permute-done((f32[16,4096]{1,0:T(8,128)S(1)}, f32[16,4096]{1,0:T(8,128)S(1)}, u32[]{:S(2)}, u32[]{:S(2)}) %collective-permute-start.1) | collective-permute-done | bytes 262176 | tf_op jit(solution)/shard_map/ppermute | solution.py:44
  46.4 0.6 %fusion.35 = f32[4096,32]{0,1:T(8,128)S(1)} fusion(f32[16,4096]{1,0:T(8,128)S(1)} %collective-permute-done.1, f32[32,16]{1,0:T(8,128)S(1)} %copy-done.6), kind=kOutput, calls=%fused_computation.50 | convolution fusion | flops 25165824 | bytes 788480 | tf_op jit(solution)/shard_map/dot_general | solution.py:180
  46.9 5.2 %collective-permute-done = f32[16,4096]{1,0:T(8,128)S(1)} collective-permute-done((f32[16,4096]{1,0:T(8,128)S(1)}, f32[16,4096]{1,0:T(8,128)S(1)}, u32[]{:S(2)}, u32[]{:S(2)}) %collective-permute-start) | collective-permute-done | bytes 262176 | tf_op jit(solution)/shard_map/ppermute | solution.py:43
  52.1 1.4 %fusion.17 = f32[32,4096]{1,0:T(8,128)} fusion(f32[4096,32]{0,1:T(8,128)S(1)} %fusion.35, f32[4096,32]{0,1:T(8,128)S(1)} %fusion.34, f32[16,4096]{1,0:T(8,128)S(1)} %collective-permute-done, f32[32,16]{1,0:T(8,128)S(1)} %copy-done.4), kind=kOutput, calls=%fused_computation.20 | convolution fusion | flops 25427968 | bytes 1837056 | tf_op jit(solution)/shard_map/dot_general | solution.py:180
  (49 shorter events, 3.8 us)
Async XLA Ops:
  0.0 0.7 %copy-start.9 = (f32[1,4,4]{2,1,0:T(4,128)S(1)}, f32[1,4,4]{2,1,0:T(4,128)}, u32[]{:S(2)}) copy-start(f32[1,4,4]{2,1,0:T(4,128)} %constant.97) | copy-start | bytes 196
  6.8 1.2 %copy-start.8 = (f32[4,128,1]{1,0,2:T(4,128)S(1)}, f32[4,128,1]{1,0,2:T(4,128)}, u32[]{:S(2)}) copy-start(f32[4,128,1]{1,0,2:T(4,128)} %constant.102) | copy-start | bytes 6148
  8.0 2.1 %copy-start.1 = (f32[128,128,1]{1,0,2:T(8,128)S(1)}, f32[128,128,1]{1,0,2:T(8,128)}, u32[]{:S(2)}) copy-start(f32[128,128,1]{1,0,2:T(8,128)} %constant.101) | copy-start | bytes 196612
  10.1 0.7 %copy-start.3 = (f32[32,4,4]{0,1,2:T(4,128)S(1)}, f32[32,4,4]{0,1,2:T(4,128)}, u32[]{:S(2)}) copy-start(f32[32,4,4]{0,1,2:T(4,128)} %constant.94.clone) | copy-start | bytes 6148
  10.1 1.0 %copy-start = (f32[32,32,4,4]{1,0,3,2:T(8,128)S(1)}, f32[32,32,4,4]{1,0,3,2:T(8,128)}, u32[]{:S(2)}) copy-start(f32[32,32,4,4]{1,0,3,2:T(8,128)} %constant.92.clone) | copy-start | bytes 196612
  17.2 0.7 %copy-start.2 = (f32[32,4,4]{0,2,1:T(4,128)S(1)}, f32[32,4,4]{0,2,1:T(4,128)}, u32[]{:S(2)}) copy-start(f32[32,4,4]{0,2,1:T(4,128)} %constant.93.clone) | copy-start | bytes 6148
  17.9 0.7 %copy-start.7 = (f32[4,128,1]{1,0,2:T(4,128)S(1)}, f32[4,128,1]{1,0,2:T(4,128)}, u32[]{:S(2)}) copy-start(f32[4,128,1]{1,0,2:T(4,128)} %constant.103) | copy-start | bytes 6148
  25.3 0.7 %copy-start.10 = (s32[32]{0:T(128)S(1)}, s32[32]{0:T(128)}, u32[]{:S(2)}) copy-start(s32[32]{0:T(128)} %param.15) | copy-start | bytes 388
  35.9 5.9 %copy-start.5 = (f32[32,32]{1,0:T(8,128)S(1)}, f32[32,32]{1,0:T(8,128)}, u32[]{:S(2)}) copy-start(f32[32,32]{1,0:T(8,128)} %constant.99) | copy-start | bytes 12292
  36.0 10.4 %collective-permute-start.1 = (f32[16,4096]{1,0:T(8,128)S(1)}, f32[16,4096]{1,0:T(8,128)S(1)}, u32[]{:S(2)}, u32[]{:S(2)}) collective-permute-start(f32[16,4096]{1,0:T(8,128)S(1)} %get-tuple-element.290), channel_id=1, source_target_pairs={{1,0},{2,1},{3,2},{4,3},{5,4},{6,5},{7,6},{9,8},{10,9},{11,10},{12... | collective-permute-start | bytes 786440 | tf_op jit(solution)/shard_map/ppermute | solution.py:44
  37.3 9.1 %copy-start.6 = (f32[32,16]{1,0:T(8,128)S(1)}, f32[32,16]{1,0:T(8,128)}, u32[]{:S(2)}) copy-start(f32[32,16]{1,0:T(8,128)} %constant.100) | copy-start | bytes 6148
  37.3 14.9 %collective-permute-start = (f32[16,4096]{1,0:T(8,128)S(1)}, f32[16,4096]{1,0:T(8,128)S(1)}, u32[]{:S(2)}, u32[]{:S(2)}) collective-permute-start(f32[16,4096]{1,0:T(8,128)S(1)} %get-tuple-element.289), channel_id=1, source_target_pairs={{0,1},{1,2},{2,3},{3,4},{4,5},{5,6},{6,7},{8,9},{9,10},{10,11},{11... | collective-permute-start | bytes 786440 | tf_op jit(solution)/shard_map/ppermute | solution.py:43
  42.4 9.7 %copy-start.4 = (f32[32,16]{1,0:T(8,128)S(1)}, f32[32,16]{1,0:T(8,128)}, u32[]{:S(2)}) copy-start(f32[32,16]{1,0:T(8,128)} %constant.98) | copy-start | bytes 6148
where the time goes:
time: 53.9 us; the launch traced here: 53.5 us
  blocking collectives  16.7 us (31%)
  matrix products  13.3 us (25%)
  waiting for transfers between devices  9.12 us (17%)
  local copies, waits for them, and re-layouts  8.16 us (15%)
  starting transfers between devices  5.85 us (11%)
    all_gather x3, blocking collectives, carried_in(): everything = jax.tree.map(lambda part: lax.all_gather(part, axis), value)  16.7 us
    ppermute x1, waiting for transfers between devices, with_halo(): before = lax.ppermute(last, axis, up)  5.19 us
    ppermute x1, starting transfers between devices, with_halo(): before = lax.ppermute(last, axis, up)  4.56 us
    dot_general x2, matrix products, local_pass(): jnp.einsum('pm,cbm->pcb', inputs_to_end, blocks, precision=highest)  4.25 us
    ppermute x1, waiting for transfers between devices, with_halo(): after = lax.ppermute(leading, axis, down)  3.93 us
    unnamed x26, local copies, waits for them, and re-layouts  3.42 us
    dot_general x3, matrix products, shards(): return jnp.dot(band_matrix, padded, precision=highest)  2.5 us
    rev x1, local copies, waits for them, and re-layouts, bandpass(): return jnp.flip(backward, axis=1)  2.33 us
  transfers between devices with their start and end apart: 2, of which 2 were waited for; matrix products, arithmetic and copies ran while one was open for 2% of the time, Pallas kernels for 0%

commit v1 on v0

v1 whole, which is shorter than its diff:
```python
import functools
import math

import jax
import jax.numpy as jnp
import numpy as np
from jax import lax
from jax.experimental import pallas as pl
from jax.experimental.pallas import tpu as pltpu
from jax.sharding import PartitionSpec as P

RADIUS = 16
BLOCK = 256
STATES = 8

low_corner = 0.015
high_corner = 100.0
sample_rate = 500.0
highest = lax.Precision.HIGHEST
VMEM = pltpu.VMEM
ANY = pl.ANY


def section(corner, highpass):
    warped = 2.0 * sample_rate * math.tan(math.pi * corner / sample_rate)
    scaled = warped / (2.0 * sample_rate * math.sqrt(2.0))
    numer_real = 1.0 - scaled
    denom_real = 1.0 + scaled
    denom_imag = -scaled
    modulus = denom_real * denom_real + denom_imag * denom_imag
    pole_real = (numer_real * denom_real + scaled * denom_imag) / modulus
    pole_imag = (scaled * denom_real - numer_real * denom_imag) / modulus
    pole_norm = pole_real * pole_real + pole_imag * pole_imag
    zero_place = 1.0 if highpass else -1.0
    section_gain = ((1.0 + zero_place * pole_real) ** 2 + pole_imag * pole_imag) / 4.0
    linear = section_gain * (2.0 * pole_real - 2.0 * zero_place)
    constant = section_gain * (1.0 - pole_norm)
    shrink = 1.0 - math.sqrt(pole_norm)
    first_out = linear / shrink
    second = (constant + pole_real * linear) / (pole_imag * shrink)
    rotation = np.array([[pole_real, -pole_imag], [pole_imag, pole_real]])
    inject = np.array([shrink, 0.0])
    return (rotation, inject, np.array([first_out, second]), section_gain)


def filter_system():
    high_rotation, high_inject, high_out, high_gain = section(low_corner, True)
    low_rotation, low_inject, low_out, low_gain = section(high_corner, False)
    upper_rows = np.concatenate([high_rotation, np.zeros((2, 2))], axis=1)
    lower_rows = np.concatenate([np.outer(low_inject, high_out), low_rotation], axis=1)
    transition = np.concatenate([upper_rows, lower_rows], axis=0)
    driving = np.concatenate([high_inject, low_inject * high_gain])
    readout = np.concatenate([high_out * low_gain, low_out])
    direct = low_gain * high_gain
    return (transition, driving, readout, direct)


def spatial_taps(extent):
    positions = np.arange(-extent, extent + 1)
    window = 0.5 * (1.0 + np.cos(np.pi * positions / (extent + 1)))
    window = window / np.sum(window)
    return np.where(positions == 0, 1.0 - window, -window)


def two_sided():
    transition, driving, readout, direct = filter_system()
    poles, vectors = np.linalg.eig(transition)
    gains = (readout @ vectors) * (np.linalg.inv(vectors) @ driving)
    pairs = 1.0 / (1.0 - poles[:, None] * poles[None, :])
    rho = direct * gains + gains * poles * (gains @ pairs)
    r0 = (direct * direct + gains @ pairs @ gains).real
    cut = -(gains / rho)[:, None] * pairs * gains[None, :]
    kept = [i for i in range(4) if poles[i].imag > 0]
    twin = [int(np.argmin(abs(poles - np.conj(poles[i])))) for i in kept]
    scale = 1.0 - abs(poles[kept])
    end = np.zeros((4, 4))
    for i, a in enumerate(kept):
        for j, (b, c) in enumerate(zip(kept, twin)):
            straight, crossed = cut[a, b], cut[a, c]
            of_real, of_imag = straight + crossed, 1j * (straight - crossed)
            ratio = scale[i] / scale[j]
            end[2 * i, 2 * j : 2 * j + 2] = of_real.real * ratio, of_imag.real * ratio
            end[2 * i + 1, 2 * j : 2 * j + 2] = of_real.imag * ratio, of_imag.imag * ratio
    return r0, rho[kept], poles[kept], scale, end


def power(poles, steps):
    out = np.zeros((4, 4))
    for i, p in enumerate(poles**steps):
        out[2 * i : 2 * i + 2, 2 * i : 2 * i + 2] = [[p.real, -p.imag], [p.imag, p.real]]
    return out


def time_tables(samples, parts):
    r0, rho, poles, scale, end = two_sided()
    blocks = samples // BLOCK
    lanes = blocks * STATES
    k = np.arange(BLOCK)
    r = np.concatenate([[r0], sum(2.0 * (c * p ** k[:-1]).real for c, p in zip(rho, poles))])
    toeplitz = r[abs(k[:, None] - k[None, :])]
    gather = np.zeros((BLOCK, STATES))
    spread = np.zeros((STATES, BLOCK))
    for i, (p, s, c) in enumerate(zip(poles, scale, rho)):
        for side, far, near in ((0, BLOCK - 1 - k, k), (4, k, BLOCK - 1 - k)):
            inject = s * p**far
            out = 2.0 * c / s * p**near
            gather[:, side + 2 * i] = inject.real
            gather[:, side + 2 * i + 1] = inject.imag
            spread[side + 2 * i] = out.real
            spread[side + 2 * i + 1] = -out.imag
    gather = np.tile(gather, (1, blocks))
    spread = np.tile(spread, (blocks, 1))
    step = [power(poles, BLOCK * m).T for m in range(blocks + 1)]
    inner = np.zeros((blocks, STATES, blocks, STATES))
    whole = np.zeros((blocks, STATES, STATES))
    carry = np.zeros((STATES, blocks, STATES))
    for b in range(blocks):
        for c in range(blocks):
            if c < b:
                inner[c, :4, b, :4] = step[b - c - 1]
            if c > b:
                inner[c, 4:, b, 4:] = step[c - b - 1]
        whole[b, :4, :4] = step[blocks - 1 - b]
        whole[b, 4:, 4:] = step[b]
        carry[:4, b, :4] = step[b]
        carry[4:, b, 4:] = step[blocks - 1 - b]
    inner = inner.reshape(lanes, lanes)
    whole = np.tile(whole.reshape(lanes, STATES), (1, blocks))
    carry = carry.reshape(STATES, lanes)
    device = [power(poles, samples * m).T for m in range(parts + 1)]
    enter = np.zeros((parts, lanes, lanes))
    for t in range(parts):
        for j in range(parts):
            at = (t - j) % parts
            into = np.zeros((STATES, STATES))
            if at < t:
                into[:4, :4] = device[t - at - 1]
            if at > t:
                into[4:, 4:] = device[at - t - 1]
            into[:4, 4:] = device[parts - 1 - at] @ end.T @ device[parts - 1 - t]
            enter[t, STATES * j : STATES * (j + 1)] = into @ carry
    return [np.asarray(v, np.float32) for v in (toeplitz, gather, spread, inner, whole, enter)]


def mix_tables(channels):
    taps = spatial_taps(RADIUS)

    def between(rows, columns):
        lag = columns[None, :] - rows[:, None]
        return np.where(abs(lag) <= RADIUS, taps[np.clip(lag + RADIUS, 0, 2 * RADIUS)], 0.0)

    mine = np.arange(channels)
    own = between(mine, mine)
    after = between(mine, channels + np.arange(RADIUS))
    before = between(mine, np.arange(-RADIUS, 0))
    both = [np.concatenate(v, axis=1) for v in ((own, after, before), (own, before, after))]
    return np.stack(both).astype(np.float32)


def halves(value):
    value = np.asarray(value, np.float32)
    high = value.astype(jnp.bfloat16)
    return high, (value - high.astype(np.float32)).astype(jnp.bfloat16)


def split(value):
    high = value.astype(jnp.bfloat16)
    return high, (value - high.astype(jnp.float32)).astype(jnp.bfloat16)


def exact(a, b):
    return jnp.dot(a, b, precision=highest, preferred_element_type=jnp.float32)


def product(a, b):
    return jnp.dot(a, b, preferred_element_type=jnp.float32)


def triple(a, high, low):
    a_high, a_low = split(a)
    return product(a_high, high) + (product(a_high, low) + product(a_low, high))


def triple_left(high, low, b):
    b_high, b_low = split(b)
    return product(high, b_high) + (product(low, b_high) + product(high, b_low))


def place():
    return lax.rem(lax.axis_index("chan"), 2)


def rows_of(x):
    return jnp.concatenate([x[:, i : i + BLOCK] for i in range(0, x.shape[1], BLOCK)], axis=0)


def keep_own(stacked, first, groups):
    rows = stacked.shape[0] // groups
    owner = lax.broadcasted_iota(jnp.int32, (rows, stacked.shape[1]), 1) // STATES
    return sum(
        jnp.where(owner == first + g, stacked[g * rows : (g + 1) * rows], 0.0)
        for g in range(groups)
    )


def spread_out(states, first, groups):
    owner = lax.broadcasted_iota(jnp.int32, states.shape, 1) // STATES
    return jnp.concatenate(
        [jnp.where(owner == first + g, states, 0.0) for g in range(groups)], axis=0
    )


def start_kernel(x_hbm, mask_hbm, gather_hbm, *refs):
    first1, second1, first2, second2, live, sums, x, mask, gather, sems = refs
    channels, samples = x.shape
    lanes = sums.shape[1]
    half = samples // 2
    parts = [pl.ds(0, half), pl.ds(half, half)]
    copies = [pltpu.make_async_copy(mask_hbm, mask, sems.at[0])]
    copies += [pltpu.make_async_copy(x_hbm.at[:, p], x.at[:, p], sems.at[1 + i]) for i, p in enumerate(parts)]
    copies += [pltpu.make_async_copy(gather_hbm, gather, sems.at[3])]
    for copy in copies:
        copy.start()
    odd = place()
    copies[0].wait()
    same = lax.broadcasted_iota(jnp.int32, (channels, channels), 0) == lax.broadcasted_iota(
        jnp.int32, (channels, channels), 1
    )
    alive = jnp.sum(
        jnp.where(same, mask[...].astype(jnp.float32), 0.0), axis=1, keepdims=True
    )
    total = jnp.zeros((channels, lanes), jnp.float32)
    for i, p in enumerate(parts):
        copies[1 + i].wait()
        here = x[:, p] * alive
        live[:, p] = here
        top, bottom = here[:RADIUS], here[channels - RADIUS :]
        to_first, to_second = jnp.where(odd == 1, top, bottom), jnp.where(odd == 1, bottom, top)
        if i == 0:
            first1[:, lanes:], second1[:, lanes:] = to_first, to_second
            copies[3].wait()
        else:
            first2[...], second2[...] = to_first, to_second
        high, low = split(rows_of(here))
        wide = product(high, gather[...])
        found = wide[:, :lanes] + wide[:, lanes:] + product(low, gather[:, :lanes])
        blocks = half // BLOCK
        total += keep_own(found, i * blocks, blocks)
    sums[...] = total
    top, bottom = total[:RADIUS], total[channels - RADIUS :]
    first1[:, :lanes] = jnp.where(odd == 1, top, bottom)
    second1[:, :lanes] = jnp.where(odd == 1, bottom, top)


def mixed_sums_kernel(sums, first1, second1, mix, out):
    lanes = sums.shape[1]
    stacked = jnp.concatenate([sums[...], first1[:, :lanes], second1[:, :lanes]], axis=0)
    out[...] = exact(mix[place()], stacked)


def early_kernel(live, first1, second1, mix, toeplitz, out):
    channels, samples = live.shape
    half = samples // 2
    lanes = first1.shape[1] - half
    high, low = split(mix[place()])
    for i in range(2):
        here = live[:, i * half : (i + 1) * half]
        if i == 0:
            here = jnp.concatenate([here, first1[:, lanes:], second1[:, lanes:]], axis=0)
            mixed = triple_left(high, low, here)
        else:
            mixed = triple_left(high[:, :channels], low[:, :channels], here)
        rows = triple(rows_of(mixed), toeplitz[:BLOCK], toeplitz[BLOCK:])
        for b in range(half // BLOCK):
            at = i * half + b * BLOCK
            out[:, at : at + BLOCK] = rows[b * channels : (b + 1) * channels]


def enter_kernel(parts, inner, whole, enter, *refs):
    sums, out = refs[:parts], refs[parts]
    stacked = jnp.concatenate([part[...] for part in sums], axis=0)
    totals = keep_own(exact(stacked, whole[...]), 0, parts)
    out[...] = exact(sums[0][...], inner[...]) + exact(totals, enter[lax.axis_index("tm")])


def finish_kernel(part, states, first2, second2, mix, toeplitz, spread, out_hbm, out, sems):
    channels, samples = part.shape
    lanes = states.shape[1]
    half = samples // 2
    blocks = half // BLOCK
    high, low = split(mix[place()][:, channels:])
    stores = []
    for i in range(2):
        rows = triple(spread_out(states[...], i * blocks, blocks), spread[:lanes], spread[lanes:])
        if i == 1:
            mixed = triple_left(high, low, jnp.concatenate([first2[...], second2[...]], axis=0))
            rows += triple(rows_of(mixed), toeplitz[:BLOCK], toeplitz[BLOCK:])
        for b in range(blocks):
            at = slice(i * half + b * BLOCK, i * half + (b + 1) * BLOCK)
            out[:, at] = part[:, at] + rows[b * channels : (b + 1) * channels]
        p = pl.ds(i * half, half)
        stores.append(pltpu.make_async_copy(out.at[:, p], out_hbm.at[:, p], sems.at[i]))
        stores[-1].start()
    for copy in stores:
        copy.wait()


def vmem(*shape, dtype=jnp.float32):
    return pltpu.VMEM(shape, dtype)


def kernel(body, name, inputs, outputs, scratch=(), cost=0, far=()):
    inputs = [
        pltpu.with_memory_space_constraint(v, pltpu.HBM if i in far else VMEM)
        for i, v in enumerate(inputs)
    ]
    out_specs = [
        pl.BlockSpec(memory_space=ANY if isinstance(o, jax.ShapeDtypeStruct) else VMEM)
        for o in outputs
    ]
    single = len(outputs) == 1
    return pl.pallas_call(
        body,
        out_shape=outputs[0] if single else tuple(outputs),
        in_specs=[pl.BlockSpec(memory_space=ANY if i in far else VMEM) for i in range(len(inputs))],
        out_specs=out_specs[0] if single else tuple(out_specs),
        scratch_shapes=list(scratch),
        compiler_params=pltpu.CompilerParams(vmem_limit_bytes=24 * 1024 * 1024),
        cost_estimate=pl.CostEstimate(flops=cost * 1000000000, bytes_accessed=0, transcendentals=0),
        name=name,
    )(*inputs)


def shards(strain, channel_mask):
    channels, samples = strain.shape
    parts = lax.axis_size("tm")
    places = lax.axis_size("chan")
    half = samples // 2
    lanes = samples // BLOCK * STATES
    toeplitz, gather, spread, inner, whole, enter = time_tables(samples, parts)
    gather = jnp.asarray(np.concatenate(halves(gather), axis=1))
    toeplitz = jnp.asarray(np.concatenate(halves(toeplitz), axis=0))
    spread = jnp.asarray(np.concatenate(halves(spread), axis=0))
    inner, whole, enter = map(jnp.asarray, (inner, whole, enter))
    mix = jnp.asarray(mix_tables(channels))

    pairs = [
        [(i + a, i + b) for i in range(start, places - 1, 2) for a, b in ((0, 1), (1, 0))]
        for start in (0, 1)
    ]
    first1, second1, first2, second2, live, sums = kernel(
        start_kernel,
        "start",
        [strain, channel_mask.reshape(1, channels), gather],
        [
            vmem(RADIUS, lanes + half),
            vmem(RADIUS, lanes + half),
            vmem(RADIUS, half),
            vmem(RADIUS, half),
            vmem(channels, samples),
            vmem(channels, lanes),
        ],
        [
            vmem(channels, samples),
            vmem(1, channels, dtype=jnp.int32),
            vmem(BLOCK, 2 * lanes, dtype=jnp.bfloat16),
            pltpu.SemaphoreType.DMA((4,)),
        ],
        far=(0, 1, 2),
    )
    first1 = lax.ppermute(first1, "chan", pairs[0])
    second1 = lax.ppermute(second1, "chan", pairs[1])
    first2 = lax.ppermute(first2, "chan", pairs[0])
    second2 = lax.ppermute(second2, "chan", pairs[1])
    sums = kernel(
        mixed_sums_kernel, "sums", [sums, first1, second1, mix], [vmem(channels, lanes)]
    )
    others = [
        lax.ppermute(sums, "tm", [(i, (i + j) % parts) for i in range(parts)])
        for j in range(1, parts)
    ]
    part = kernel(
        early_kernel, "early", [live, first1, second1, mix, toeplitz], [vmem(channels, samples)]
    )
    states = kernel(
        functools.partial(enter_kernel, parts),
        "enter",
        [inner, whole, enter, sums, *others],
        [vmem(channels, lanes)],
    )
    return kernel(
        finish_kernel,
        "finish",
        [part, states, first2, second2, mix, toeplitz, spread],
        [jax.ShapeDtypeStruct((channels, samples), jnp.float32)],
        [vmem(channels, samples), pltpu.SemaphoreType.DMA((2,))],
    )


def solution(mesh):
    placed = (P("chan", "tm"), P("chan"))
    return jax.shard_map(
        shards, mesh=mesh, in_specs=placed, out_specs=P("chan", "tm"), check_vma=False
    )
```

time: 53.9 us -> 19.3 us (0.36)
  the two profiles are of different devices: /device:TPU:0 before, /device:TPU:24 now
where the time goes in v1:
time: 19.3 us; the launch traced here: 19.1 us
  starting transfers between devices  10.1 us (52%)
  Pallas kernels  4.72 us (24%)
  waiting for transfers between devices  4.14 us (21%)
    pallas_call x5, Pallas kernels, kernel(): pl.pallas_call(body, out_shape=outputs[0] if single else tuple(outputs),...  4.72 us
    ppermute x1, starting transfers between devices, shards(): second2 = lax.ppermute(second2, 'chan', pairs[1])  4.41 us
    ppermute x1, starting transfers between devices, shards(): second1 = lax.ppermute(second1, 'chan', pairs[1])  2.32 us
    ppermute x1, waiting for transfers between devices, shards(): second1 = lax.ppermute(second1, 'chan', pairs[1])  2.12 us
    ppermute x3, waiting for transfers between devices, shards(): lax.ppermute(sums, 'tm', [(i, (i + j) % parts) for i in range(parts)])  2 us
    ppermute x3, starting transfers between devices, shards(): lax.ppermute(sums, 'tm', [(i, (i + j) % parts) for i in range(parts)])  1.76 us
    ppermute x1, starting transfers between devices, shards(): first1 = lax.ppermute(first1, 'chan', pairs[0])  1.56 us
  transfers between devices with their start and end apart: 7, of which 3 were waited for; matrix products, arithmetic and copies ran while one was open for 0% of the time, Pallas kernels for 8%

profile of v1, /device:TPU:24, one launch (start us, length us, event | category | flops | bytes accessed | tf_op | source)
XLA Modules:
  0.0 19.1 jit_solution(10748280677090220377)
XLA Ops:
  0.0 1.6 %start.1 = (f32[16,2176]{1,0:T(8,128)S(1)}, f32[16,2176]{1,0:T(8,128)S(1)}, f32[16,2048]{1,0:T(8,128)S(1)}, f32[16,2048]{1,0:T(8,128)S(1)}, f32[32,4096]{1,0:T(8,128)S(1)}, /*index=5*/f32[32,128]{1,0:T(8,128)S(1)}) custom-call(f32[32,4096]{1,0:T(8,128)} %x_hbm.1, s32[1,32]{1,0:T(1,128)} %bitcast.1, bf16[256,256]{1,0:T(8,128)(2,1)} %constant.14.clone.gather_hbm), custom_call_target="tpu_custom_call" | custom-call | tf_op jit(solution)/shard_map/start/pallas_call | solution.py:322
  1.6 0.0 copy-start
  1.6 1.6 %collective-permute-start = (f32[16,2176]{1,0:T(8,128)S(1)}, f32[16,2176]{1,0:T(8,128)S(1)}, u32[]{:S(2)}, u32[]{:S(2)}) collective-permute-start(f32[16,2176]{1,0:T(8,128)S(1)} %get-tuple-element.12), channel_id=1, source_target_pairs={{0,1},{1,0},{2,3},{3,2},{4,5},{5,4},{6,7},{7,6},{8,9},{9,8},{10,11... | collective-permute-start | bytes 417800 | tf_op jit(solution)/shard_map/ppermute | solution.py:371
  3.2 2.3 %collective-permute-start.1 = (f32[16,2176]{1,0:T(8,128)S(1)}, f32[16,2176]{1,0:T(8,128)S(1)}, u32[]{:S(2)}, u32[]{:S(2)}) collective-permute-start(f32[16,2176]{1,0:T(8,128)S(1)} %get-tuple-element.13), channel_id=1, source_target_pairs={{1,2},{2,1},{3,4},{4,3},{5,6},{6,5},{9,10},{10,9},{11,12},{12,11},... | collective-permute-start | bytes 417800 | tf_op jit(solution)/shard_map/ppermute | solution.py:372
  5.5 0.1 collective-permute-start.5
  5.6 4.4 %collective-permute-start.6 = (f32[16,2048]{1,0:T(8,128)S(1)}, f32[16,2048]{1,0:T(8,128)S(1)}, u32[]{:S(2)}, u32[]{:S(2)}) collective-permute-start(f32[16,2048]{1,0:T(8,128)S(1)} %get-tuple-element.16), channel_id=1, source_target_pairs={{1,2},{2,1},{3,4},{4,3},{5,6},{6,5},{9,10},{10,9},{11,12},{12,11},... | collective-permute-start | bytes 393224 | tf_op jit(solution)/shard_map/ppermute | solution.py:374
  10.0 0.0 collective-permute-done.first1
  10.0 2.1 %collective-permute-done.1.second1 = f32[16,2176]{1,0:T(8,128)S(1)} collective-permute-done((f32[16,2176]{1,0:T(8,128)S(1)}, f32[16,2176]{1,0:T(8,128)S(1)}, u32[]{:S(2)}, u32[]{:S(2)}) %collective-permute-start.1) | collective-permute-done | bytes 139296 | tf_op jit(solution)/shard_map/ppermute | solution.py:372
  12.1 0.0 copy-done.1
  12.1 0.1 sums.1.refs_0_
  12.3 0.0 collective-permute-start.4
  12.3 1.6 %collective-permute-start.3 = (f32[32,128]{1,0:T(8,128)S(1)}, f32[32,128]{1,0:T(8,128)S(1)}, u32[]{:S(2)}, u32[]{:S(2)}) collective-permute-start(f32[32,128]{1,0:T(8,128)S(1)} %sums.1.refs_0_), channel_id=1, source_target_pairs={{0,16},{8,24},{16,0},{24,8},{1,17},{9,25},{17,1},{25,9},{2,18},{10... | collective-permute-start | bytes 49160 | tf_op jit(solution)/shard_map/ppermute | solution.py:379
  13.9 0.2 collective-permute-start.2
  14.0 0.0 copy-done
  14.0 0.9 %early.1.part = f32[32,4096]{1,0:T(8,128)S(1)} custom-call(f32[32,4096]{1,0:T(8,128)S(1)} %get-tuple-element.11.live, f32[16,2176]{1,0:T(8,128)S(1)} %collective-permute-done.first1, f32[16,2176]{1,0:T(8,128)S(1)} %collective-permute-done.1.second1, f32[2,32,64]{2,1,0:T(8,128)S(1)} %copy-done.1, bf16[512,256]{1,0:T(8,128)(2,1)S(1)} %copy-done), custom_call_target="tpu_custom_call" | custom-call | tf_op jit(solution)/shard_map/early/pallas_call | solution.py:322
  15.0 0.0 copy-start.3
  15.0 0.0 collective-permute-done.4.refs_3_
  15.0 1.0 %collective-permute-done.3.refs_2_ = f32[32,128]{1,0:T(8,128)S(1)} collective-permute-done((f32[32,128]{1,0:T(8,128)S(1)}, f32[32,128]{1,0:T(8,128)S(1)}, u32[]{:S(2)}, u32[]{:S(2)}) %collective-permute-start.3) | collective-permute-done | bytes 16416 | tf_op jit(solution)/shard_map/ppermute | solution.py:379
  16.1 0.9 %collective-permute-done.2.refs_1_ = f32[32,128]{1,0:T(8,128)S(1)} collective-permute-done((f32[32,128]{1,0:T(8,128)S(1)}, f32[32,128]{1,0:T(8,128)S(1)}, u32[]{:S(2)}, u32[]{:S(2)}) %collective-permute-start.2) | collective-permute-done | bytes 16416 | tf_op jit(solution)/shard_map/ppermute | solution.py:379
  17.0 0.0 copy-done.2
  17.0 0.5 %enter.2.states = f32[32,128]{1,0:T(8,128)S(1)} custom-call(f32[128,128]{1,0:T(8,128)S(1)} %copy-done.5, f32[128,128]{1,0:T(8,128)S(1)} %copy-done.4, f32[4,128,128]{2,1,0:T(8,128)S(1)} %copy-done.2, f32[32,128]{1,0:T(8,128)S(1)} %sums.1.refs_0_, f32[32,128]{1,0:T(8,128)S(1)} %collective-permute-done.2.refs_1_, ...), custom_call_target="tpu_custom_call" | custom-call | tf_op jit(solution)/shard_map/enter/pallas_call | solution.py:322
  17.5 0.0 collective-permute-done.5.first2
  17.5 0.0 collective-permute-done.6.second2
  17.5 1.6 %finish.1 = f32[32,4096]{1,0:T(8,128)} custom-call(f32[32,4096]{1,0:T(8,128)S(1)} %early.1.part, f32[32,128]{1,0:T(8,128)S(1)} %enter.2.states, f32[16,2048]{1,0:T(8,128)S(1)} %collective-permute-done.5.first2, f32[16,2048]{1,0:T(8,128)S(1)} %collective-permute-done.6.second2, f32[2,32,64]{2,1,0:T(8,128)S(1)} %copy-done.1, bf16[512,256]{1,0:T(8,128)(2,1)S(1)} %copy-done, ...), custom_call_target="tpu_custom_call" | custom-call | tf_op jit(solution)/shard_map/finish/pallas_call | solution.py:322
  (7 shorter events, 0.0 us)
Async XLA Ops:
  0.0 12.1 %copy-start.1 = (f32[2,32,64]{2,1,0:T(8,128)S(1)}, f32[2,32,64]{2,1,0:T(8,128)}, u32[]{:S(2)}) copy-start(f32[2,32,64]{2,1,0:T(8,128)} %constant.20.clone.mix) | copy-start | bytes 49156
  1.6 12.4 %copy-start = (bf16[512,256]{1,0:T(8,128)(2,1)S(1)}, bf16[512,256]{1,0:T(8,128)(2,1)}, u32[]{:S(2)}) copy-start(bf16[512,256]{1,0:T(8,128)(2,1)} %constant.15.clone.toeplitz) | copy-start | bytes 786436
  1.6 8.4 %collective-permute-start = (f32[16,2176]{1,0:T(8,128)S(1)}, f32[16,2176]{1,0:T(8,128)S(1)}, u32[]{:S(2)}, u32[]{:S(2)}) collective-permute-start(f32[16,2176]{1,0:T(8,128)S(1)} %get-tuple-element.12), channel_id=1, source_target_pairs={{0,1},{1,0},{2,3},{3,2},{4,5},{5,4},{6,7},{7,6},{8,9},{9,8},{10,11... | collective-permute-start | bytes 417800 | tf_op jit(solution)/shard_map/ppermute | solution.py:371
  3.2 9.0 %collective-permute-start.1 = (f32[16,2176]{1,0:T(8,128)S(1)}, f32[16,2176]{1,0:T(8,128)S(1)}, u32[]{:S(2)}, u32[]{:S(2)}) collective-permute-start(f32[16,2176]{1,0:T(8,128)S(1)} %get-tuple-element.13), channel_id=1, source_target_pairs={{1,2},{2,1},{3,4},{4,3},{5,6},{6,5},{9,10},{10,9},{11,12},{12,11},... | collective-permute-start | bytes 417800 | tf_op jit(solution)/shard_map/ppermute | solution.py:372
  5.5 12.0 %collective-permute-start.5 = (f32[16,2048]{1,0:T(8,128)S(1)}, f32[16,2048]{1,0:T(8,128)S(1)}, u32[]{:S(2)}, u32[]{:S(2)}) collective-permute-start(f32[16,2048]{1,0:T(8,128)S(1)} %get-tuple-element.15), channel_id=1, source_target_pairs={{0,1},{1,0},{2,3},{3,2},{4,5},{5,4},{6,7},{7,6},{8,9},{9,8},{10,11... | collective-permute-start | bytes 393224 | tf_op jit(solution)/shard_map/ppermute | solution.py:373
  5.6 11.9 %collective-permute-start.6 = (f32[16,2048]{1,0:T(8,128)S(1)}, f32[16,2048]{1,0:T(8,128)S(1)}, u32[]{:S(2)}, u32[]{:S(2)}) collective-permute-start(f32[16,2048]{1,0:T(8,128)S(1)} %get-tuple-element.16), channel_id=1, source_target_pairs={{1,2},{2,1},{3,4},{4,3},{5,6},{6,5},{9,10},{10,9},{11,12},{12,11},... | collective-permute-start | bytes 393224 | tf_op jit(solution)/shard_map/ppermute | solution.py:374
  12.3 2.7 %collective-permute-start.4 = (f32[32,128]{1,0:T(8,128)S(1)}, f32[32,128]{1,0:T(8,128)S(1)}, u32[]{:S(2)}, u32[]{:S(2)}) collective-permute-start(f32[32,128]{1,0:T(8,128)S(1)} %sums.1.refs_0_), channel_id=1, source_target_pairs={{0,24},{8,0},{16,8},{24,16},{1,25},{9,1},{17,9},{25,17},{2,26},{10... | collective-permute-start | bytes 49160 | tf_op jit(solution)/shard_map/ppermute | solution.py:379
  12.3 3.8 %collective-permute-start.3 = (f32[32,128]{1,0:T(8,128)S(1)}, f32[32,128]{1,0:T(8,128)S(1)}, u32[]{:S(2)}, u32[]{:S(2)}) collective-permute-start(f32[32,128]{1,0:T(8,128)S(1)} %sums.1.refs_0_), channel_id=1, source_target_pairs={{0,16},{8,24},{16,0},{24,8},{1,17},{9,25},{17,1},{25,9},{2,18},{10... | collective-permute-start | bytes 49160 | tf_op jit(solution)/shard_map/ppermute | solution.py:379
  13.9 3.2 %collective-permute-start.2 = (f32[32,128]{1,0:T(8,128)S(1)}, f32[32,128]{1,0:T(8,128)S(1)}, u32[]{:S(2)}, u32[]{:S(2)}) collective-permute-start(f32[32,128]{1,0:T(8,128)S(1)} %sums.1.refs_0_), channel_id=1, source_target_pairs={{0,8},{8,16},{16,24},{24,0},{1,9},{9,17},{17,25},{25,1},{2,10},{10... | collective-permute-start | bytes 49160 | tf_op jit(solution)/shard_map/ppermute | solution.py:379
  14.0 3.0 %copy-start.2 = (f32[4,128,128]{2,1,0:T(8,128)S(1)}, f32[4,128,128]{2,1,0:T(8,128)}, u32[]{:S(2)}) copy-start(f32[4,128,128]{2,1,0:T(8,128)} %constant.19.clone.enter) | copy-start | bytes 786436
  14.0 3.0 %copy-start.4 = (f32[128,128]{1,0:T(8,128)S(1)}, f32[128,128]{1,0:T(8,128)}, u32[]{:S(2)}) copy-start(f32[128,128]{1,0:T(8,128)} %constant.18.clone.whole) | copy-start | bytes 196612
  14.0 3.0 %copy-start.5 = (f32[128,128]{1,0:T(8,128)S(1)}, f32[128,128]{1,0:T(8,128)}, u32[]{:S(2)}) copy-start(f32[128,128]{1,0:T(8,128)} %constant.17.clone.inner) | copy-start | bytes 196612
  15.0 2.5 %copy-start.3 = (bf16[256,256]{1,0:T(8,128)(2,1)S(1)}, bf16[256,256]{1,0:T(8,128)(2,1)}, u32[]{:S(2)}) copy-start(bf16[256,256]{1,0:T(8,128)(2,1)} %constant.16.clone.spread) | copy-start | bytes 393220

commit v2 on v1

--- a/solution.py
+++ b/solution.py
@@ -12,6 +12,7 @@
 RADIUS = 16
 BLOCK = 256
 STATES = 8
+SUMS_COST = 0
 
 low_corner = 0.015
 high_corner = 100.0
@@ -125,10 +126,10 @@
         carry[:4, b, :4] = step[b]
         carry[4:, b, 4:] = step[blocks - 1 - b]
     inner = inner.reshape(lanes, lanes)
-    whole = np.tile(whole.reshape(lanes, STATES), (1, blocks))
+    whole = whole.reshape(lanes, STATES).T
     carry = carry.reshape(STATES, lanes)
     device = [power(poles, samples * m).T for m in range(parts + 1)]
-    enter = np.zeros((parts, lanes, lanes))
+    enter = np.zeros((parts, parts * STATES, lanes))
     for t in range(parts):
         for j in range(parts):
             at = (t - j) % parts
@@ -176,14 +177,18 @@
     return jnp.dot(a, b, preferred_element_type=jnp.float32)
 
 
-def triple(a, high, low):
-    a_high, a_low = split(a)
-    return product(a_high, high) + (product(a_high, low) + product(a_low, high))
-
-
-def triple_left(high, low, b):
-    b_high, b_low = split(b)
-    return product(high, b_high) + (product(low, b_high) + product(high, b_low))
+def mixing(weights, x):
+    a, b = split(weights)
+    high, low = split(x)
+    return product(jnp.concatenate([a, b, a], axis=1), jnp.concatenate([high, high, low], axis=0))
+
+
+def filtering(rows, toeplitz):
+    high, low = split(rows)
+    above, below = toeplitz[:BLOCK], toeplitz[BLOCK:]
+    return product(
+        jnp.concatenate([high, high, low], axis=1), jnp.concatenate([above, below, above], axis=0)
+    )
 
 
 def place():
@@ -194,31 +199,33 @@
     return jnp.concatenate([x[:, i : i + BLOCK] for i in range(0, x.shape[1], BLOCK)], axis=0)
 
 
-def keep_own(stacked, first, groups):
+def keep_own(stacked, groups):
     rows = stacked.shape[0] // groups
     owner = lax.broadcasted_iota(jnp.int32, (rows, stacked.shape[1]), 1) // STATES
     return sum(
-        jnp.where(owner == first + g, stacked[g * rows : (g + 1) * rows], 0.0)
-        for g in range(groups)
-    )
-
-
-def spread_out(states, first, groups):
+        jnp.where(owner == g, stacked[g * rows : (g + 1) * rows], 0.0) for g in range(groups)
+    )
+
+
+def spreading(states, first, groups, spread):
+    lanes = states.shape[1]
     owner = lax.broadcasted_iota(jnp.int32, states.shape, 1) // STATES
-    return jnp.concatenate(
-        [jnp.where(owner == first + g, states, 0.0) for g in range(groups)], axis=0
-    )
-
-
-def start_kernel(x_hbm, mask_hbm, gather_hbm, *refs):
+    rows = [jnp.where(owner == first + g, states, 0.0) for g in range(groups)]
+    high, low = split(jnp.concatenate(rows, axis=0))
+    above, below = spread[:lanes], spread[lanes:]
+    return product(
+        jnp.concatenate([high, low], axis=1), jnp.concatenate([above, above], axis=0)
+    ) + product(high, below)
+
+
+def start_kernel(cuts, x_hbm, mask_hbm, gather_hbm, *refs):
     first1, second1, first2, second2, live, sums, x, mask, gather, sems = refs
-    channels, samples = x.shape
+    channels = x.shape[0]
     lanes = sums.shape[1]
-    half = samples // 2
-    parts = [pl.ds(0, half), pl.ds(half, half)]
-    copies = [pltpu.make_async_copy(mask_hbm, mask, sems.at[0])]
-    copies += [pltpu.make_async_copy(x_hbm.at[:, p], x.at[:, p], sems.at[1 + i]) for i, p in enumerate(parts)]
-    copies += [pltpu.make_async_copy(gather_hbm, gather, sems.at[3])]
+    copies = [
+        pltpu.make_async_copy(source, target, sems.at[i])
+        for i, (source, target) in enumerate([(mask_hbm, mask), (gather_hbm, gather), (x_hbm, x)])
+    ]
     for copy in copies:
         copy.start()
     odd = place()
@@ -229,76 +236,84 @@
     alive = jnp.sum(
         jnp.where(same, mask[...].astype(jnp.float32), 0.0), axis=1, keepdims=True
     )
-    total = jnp.zeros((channels, lanes), jnp.float32)
-    for i, p in enumerate(parts):
-        copies[1 + i].wait()
-        here = x[:, p] * alive
-        live[:, p] = here
-        top, bottom = here[:RADIUS], here[channels - RADIUS :]
-        to_first, to_second = jnp.where(odd == 1, top, bottom), jnp.where(odd == 1, bottom, top)
-        if i == 0:
-            first1[:, lanes:], second1[:, lanes:] = to_first, to_second
-            copies[3].wait()
-        else:
-            first2[...], second2[...] = to_first, to_second
-        high, low = split(rows_of(here))
-        wide = product(high, gather[...])
-        found = wide[:, :lanes] + wide[:, lanes:] + product(low, gather[:, :lanes])
-        blocks = half // BLOCK
-        total += keep_own(found, i * blocks, blocks)
+    copies[1].wait()
+    copies[2].wait()
+    here = x[...] * alive
+    live[...] = here
+
+    def send(value, first, second):
+        top, bottom = value[:RADIUS], value[channels - RADIUS :]
+        for out, even_rows, odd_rows in ((first, bottom, top), (second, top, bottom)):
+            rows = jnp.where(odd == 1, odd_rows, even_rows)
+            start = 0
+            for ref, at, stop in out:
+                if stop > start:
+                    ref[:, at : at + stop - start] = rows[:, start:stop]
+                start = stop
+
+    samples = here.shape[1]
+    send(
+        here,
+        [(first1, lanes, cuts[0]), (first2, 0, samples)],
+        [(second1, lanes, cuts[1]), (second2, 0, samples)],
+    )
+    high, low = split(rows_of(here))
+    wide = product(high, gather[...])
+    found = wide[:, :lanes] + wide[:, lanes:] + product(low, gather[:, :lanes])
+    total = keep_own(found, samples // BLOCK)
     sums[...] = total
-    top, bottom = total[:RADIUS], total[channels - RADIUS :]
-    first1[:, :lanes] = jnp.where(odd == 1, top, bottom)
-    second1[:, :lanes] = jnp.where(odd == 1, bottom, top)
-
-
-def mixed_sums_kernel(sums, first1, second1, mix, out):
+    send(total, [(first1, 0, lanes)], [(second1, 0, lanes)])
+
+
+def sums_kernel(sums, first1, second1, mix, whole, out, device_out):
     lanes = sums.shape[1]
     stacked = jnp.concatenate([sums[...], first1[:, :lanes], second1[:, :lanes]], axis=0)
-    out[...] = exact(mix[place()], stacked)
-
-
-def early_kernel(live, first1, second1, mix, toeplitz, out):
+    total = exact(mix[place()], stacked)
+    out[...] = total
+    device_out[...] = lax.dot_general(
+        whole[...], total, (((1,), (1,)), ((), ())), precision=highest
+    )
+
+
+def padded(value, before, after):
+    rows = value.shape[0]
+    sides = [jnp.zeros((rows, n), jnp.float32) if n else None for n in (before, after)]
+    return jnp.concatenate([v for v in (sides[0], value, sides[1]) if v is not None], axis=1)
+
+
+def early_kernel(live, first1, second1, sums, mix, toeplitz, inner, out, states):
     channels, samples = live.shape
-    half = samples // 2
-    lanes = first1.shape[1] - half
-    high, low = split(mix[place()])
-    for i in range(2):
-        here = live[:, i * half : (i + 1) * half]
-        if i == 0:
-            here = jnp.concatenate([here, first1[:, lanes:], second1[:, lanes:]], axis=0)
-            mixed = triple_left(high, low, here)
-        else:
-            mixed = triple_left(high[:, :channels], low[:, :channels], here)
-        rows = triple(rows_of(mixed), toeplitz[:BLOCK], toeplitz[BLOCK:])
-        for b in range(half // BLOCK):
-            at = i * half + b * BLOCK
-            out[:, at : at + BLOCK] = rows[b * channels : (b + 1) * channels]
-
-
-def enter_kernel(parts, inner, whole, enter, *refs):
-    sums, out = refs[:parts], refs[parts]
-    stacked = jnp.concatenate([part[...] for part in sums], axis=0)
-    totals = keep_own(exact(stacked, whole[...]), 0, parts)
-    out[...] = exact(sums[0][...], inner[...]) + exact(totals, enter[lax.axis_index("tm")])
-
-
-def finish_kernel(part, states, first2, second2, mix, toeplitz, spread, out_hbm, out, sems):
+    lanes = sums.shape[1]
+    states[...] = exact(sums[...], inner[...])
+    edges = [padded(ref[:, lanes:], 0, samples + lanes - ref.shape[1]) for ref in (first1, second1)]
+    mixed = mixing(mix[place()], jnp.concatenate([live[...], *edges], axis=0))
+    rows = filtering(rows_of(mixed), toeplitz[...])
+    for b in range(samples // BLOCK):
+        out[:, b * BLOCK : (b + 1) * BLOCK] = rows[b * channels : (b + 1) * channels]
+
+
+def finish_kernel(cuts, part, states, first2, second2, mix, toeplitz, enter, spread, *refs):
+    devices, (out_hbm, out, sems) = refs[:-3], refs[-3:]
     channels, samples = part.shape
-    lanes = states.shape[1]
-    half = samples // 2
-    blocks = half // BLOCK
-    high, low = split(mix[place()][:, channels:])
+    cut = min(cuts)
+    at = lax.axis_index("tm")
+    arrived = jnp.concatenate([ref[...] for ref in devices], axis=0)
+    inside = states[...] + lax.dot_general(
+        arrived, enter[at], (((0,), (0,)), ((), ())), precision=highest
+    )
+    weights = mix[place()][:, channels:]
     stores = []
-    for i in range(2):
-        rows = triple(spread_out(states[...], i * blocks, blocks), spread[:lanes], spread[lanes:])
+    for i, (start, stop) in enumerate(((0, cut), (cut, samples))):
+        groups = (stop - start) // BLOCK
+        rows = spreading(inside, start // BLOCK, groups, spread[...])
         if i == 1:
-            mixed = triple_left(high, low, jnp.concatenate([first2[...], second2[...]], axis=0))
-            rows += triple(rows_of(mixed), toeplitz[:BLOCK], toeplitz[BLOCK:])
-        for b in range(blocks):
-            at = slice(i * half + b * BLOCK, i * half + (b + 1) * BLOCK)
-            out[:, at] = part[:, at] + rows[b * channels : (b + 1) * channels]
-        p = pl.ds(i * half, half)
+            edges = [padded(ref[...], stop - start - ref.shape[1], 0) for ref in (first2, second2)]
+            mixed = mixing(weights, jnp.concatenate(edges, axis=0))
+            rows += filtering(rows_of(mixed), toeplitz[...])
+        for b in range(groups):
+            here = slice(start + b * BLOCK, start + (b + 1) * BLOCK)
+            out[:, here] = part[:, here] + rows[b * channels : (b + 1) * channels]
+        p = pl.ds(start, stop - start)
         stores.append(pltpu.make_async_copy(out.at[:, p], out_hbm.at[:, p], sems.at[i]))
         stores[-1].start()
     for copy in stores:
@@ -335,8 +350,8 @@
     channels, samples = strain.shape
     parts = lax.axis_size("tm")
     places = lax.axis_size("chan")
-    half = samples // 2
     lanes = samples // BLOCK * STATES
+    cuts = (samples // 2, samples // 2)
     toeplitz, gather, spread, inner, whole, enter = time_tables(samples, parts)
     gather = jnp.asarray(np.concatenate(halves(gather), axis=1))
     toeplitz = jnp.asarray(np.concatenate(halves(toeplitz), axis=0))
@@ -349,14 +364,14 @@
         for start in (0, 1)
     ]
     first1, second1, first2, second2, live, sums = kernel(
-        start_kernel,
+        functools.partial(start_kernel, cuts),
         "start",
         [strain, channel_mask.reshape(1, channels), gather],
         [
-            vmem(RADIUS, lanes + half),
-            vmem(RADIUS, lanes + half),
-            vmem(RADIUS, half),
-            vmem(RADIUS, half),
+            vmem(RADIUS, lanes + cuts[0]),
+            vmem(RADIUS, lanes + cuts[1]),
+            vmem(RADIUS, samples - cuts[0]),
+            vmem(RADIUS, samples - cuts[1]),
             vmem(channels, samples),
             vmem(channels, lanes),
         ],
@@ -364,7 +379,7 @@
             vmem(channels, samples),
             vmem(1, channels, dtype=jnp.int32),
             vmem(BLOCK, 2 * lanes, dtype=jnp.bfloat16),
-            pltpu.SemaphoreType.DMA((4,)),
+            pltpu.SemaphoreType.DMA((3,)),
         ],
         far=(0, 1, 2),
     )
@@ -372,26 +387,27 @@
     second1 = lax.ppermute(second1, "chan", pairs[1])
     first2 = lax.ppermute(first2, "chan", pairs[0])
     second2 = lax.ppermute(second2, "chan", pairs[1])
-    sums = kernel(
-        mixed_sums_kernel, "sums", [sums, first1, second1, mix], [vmem(channels, lanes)]
+    sums, device = kernel(
+        sums_kernel,
+        "sums",
+        [sums, first1, second1, mix, whole],
+        [vmem(channels, lanes), vmem(STATES, channels)],
+        cost=SUMS_COST,
     )
     others = [
-        lax.ppermute(sums, "tm", [(i, (i + j) % parts) for i in range(parts)])
+        lax.ppermute(device, "tm", [(i, (i + j) % parts) for i in range(parts)])
         for j in range(1, parts)
     ]
-    part = kernel(
-        early_kernel, "early", [live, first1, second1, mix, toeplitz], [vmem(channels, samples)]
-    )
-    states = kernel(
-        functools.partial(enter_kernel, parts),
-        "enter",
-        [inner, whole, enter, sums, *others],
-        [vmem(channels, lanes)],
+    part, states = kernel(
+        early_kernel,
+        "early",
+        [live, first1, second1, sums, mix, toeplitz, inner],
+        [vmem(channels, samples), vmem(channels, lanes)],
     )
     return kernel(
-        finish_kernel,
+        functools.partial(finish_kernel, cuts),
         "finish",
-        [part, states, first2, second2, mix, toeplitz, spread],
+        [part, states, first2, second2, mix, toeplitz, enter, spread, device, *others],
         [jax.ShapeDtypeStruct((channels, samples), jnp.float32)],
         [vmem(channels, samples), pltpu.SemaphoreType.DMA((2,))],
     )

time: 19.3 us -> 18.7 us (0.969)
  Pallas kernels: 4.72 us -> 4.13 us
    ppermute x1, waiting for transfers between devices: 0.01 us -> 1.12 us  [shards(): first2 = lax.ppermute(first2, 'chan', pairs[0])]
    ppermute x3, waiting for transfers between devices: 2 us -> 0.98 us  [shards(): lax.ppermute(device, 'tm', [(i, (i + j) % parts) for i in range(parts)])]
    pallas_call x5 -> x4, Pallas kernels: 4.72 us -> 4.13 us  [kernel(): pl.pallas_call(body, out_shape=outputs[0] if single else tuple(outputs),...]
  transfers between devices with their start and end apart: 7 -> 7, of which waited for: 3 -> 3; matrix products, arithmetic and copies ran while one was open for 0% -> 0% of each run, Pallas kernels for 8% -> 5%
where the time goes in v2:
time: 18.7 us; the launch traced here: 18.6 us
  starting transfers between devices  10.1 us (54%)
  waiting for transfers between devices  4.22 us (23%)
  Pallas kernels  4.13 us (22%)
    ppermute x1, starting transfers between devices, shards(): second2 = lax.ppermute(second2, 'chan', pairs[1])  4.41 us
    pallas_call x4, Pallas kernels, kernel(): pl.pallas_call(body, out_shape=outputs[0] if single else tuple(outputs),...  4.13 us
    ppermute x1, starting transfers between devices, shards(): second1 = lax.ppermute(second1, 'chan', pairs[1])  2.32 us
    ppermute x1, waiting for transfers between devices, shards(): second1 = lax.ppermute(second1, 'chan', pairs[1])  2.12 us
    ppermute x3, starting transfers between devices, shards(): lax.ppermute(device, 'tm', [(i, (i + j) % parts) for i in range(parts)])  1.76 us
    ppermute x1, starting transfers between devices, shards(): first1 = lax.ppermute(first1, 'chan', pairs[0])  1.56 us
    ppermute x1, waiting for transfers between devices, shards(): first2 = lax.ppermute(first2, 'chan', pairs[0])  1.12 us
    ppermute x3, waiting for transfers between devices, shards(): lax.ppermute(device, 'tm', [(i, (i + j) % parts) for i in range(parts)])  0.98 us
  transfers between devices with their start and end apart: 7, of which 3 were waited for; matrix products, arithmetic and copies ran while one was open for 0% of the time, Pallas kernels for 5%

profile of v2, /device:TPU:24, one launch (start us, length us, event | category | flops | bytes accessed | tf_op | source)
XLA Modules:
  0.0 18.6 jit_solution(3734616558523672655)
XLA Ops:
  0.0 1.5 %start.1 = (f32[16,2176]{1,0:T(8,128)S(1)}, f32[16,2176]{1,0:T(8,128)S(1)}, f32[16,2048]{1,0:T(8,128)S(1)}, f32[16,2048]{1,0:T(8,128)S(1)}, f32[32,4096]{1,0:T(8,128)S(1)}, /*index=5*/f32[32,128]{1,0:T(8,128)S(1)}) custom-call(f32[32,4096]{1,0:T(8,128)} %x_hbm.1, s32[1,32]{1,0:T(1,128)} %bitcast.1, bf16[256,256]{1,0:T(8,128)(2,1)} %constant.14.clone.gather_hbm), custom_call_target="tpu_custom_call" | custom-call | tf_op jit(solution)/shard_map/start/pallas_call | solution.py:337
  1.5 0.0 copy-start
  1.5 1.6 %collective-permute-start = (f32[16,2176]{1,0:T(8,128)S(1)}, f32[16,2176]{1,0:T(8,128)S(1)}, u32[]{:S(2)}, u32[]{:S(2)}) collective-permute-start(f32[16,2176]{1,0:T(8,128)S(1)} %get-tuple-element.16), channel_id=1, source_target_pairs={{0,1},{1,0},{2,3},{3,2},{4,5},{5,4},{6,7},{7,6},{8,9},{9,8},{10,11... | collective-permute-start | bytes 417800 | tf_op jit(solution)/shard_map/ppermute | solution.py:386
  3.1 2.3 %collective-permute-start.1 = (f32[16,2176]{1,0:T(8,128)S(1)}, f32[16,2176]{1,0:T(8,128)S(1)}, u32[]{:S(2)}, u32[]{:S(2)}) collective-permute-start(f32[16,2176]{1,0:T(8,128)S(1)} %get-tuple-element.17), channel_id=1, source_target_pairs={{1,2},{2,1},{3,4},{4,3},{5,6},{6,5},{9,10},{10,9},{11,12},{12,11},... | collective-permute-start | bytes 417800 | tf_op jit(solution)/shard_map/ppermute | solution.py:387
  5.4 0.1 collective-permute-start.2
  5.5 4.4 %collective-permute-start.3 = (f32[16,2048]{1,0:T(8,128)S(1)}, f32[16,2048]{1,0:T(8,128)S(1)}, u32[]{:S(2)}, u32[]{:S(2)}) collective-permute-start(f32[16,2048]{1,0:T(8,128)S(1)} %get-tuple-element.23), channel_id=1, source_target_pairs={{1,2},{2,1},{3,4},{4,3},{5,6},{6,5},{9,10},{10,9},{11,12},{12,11},... | collective-permute-start | bytes 393224 | tf_op jit(solution)/shard_map/ppermute | solution.py:389
  9.9 0.0 collective-permute-done.first1
  9.9 2.1 %collective-permute-done.1.second1 = f32[16,2176]{1,0:T(8,128)S(1)} collective-permute-done((f32[16,2176]{1,0:T(8,128)S(1)}, f32[16,2176]{1,0:T(8,128)S(1)}, u32[]{:S(2)}, u32[]{:S(2)}) %collective-permute-start.1) | collective-permute-done | bytes 139296 | tf_op jit(solution)/shard_map/ppermute | solution.py:387
  12.0 0.0 copy-done.1
  12.0 0.0 copy-done.5
  12.0 0.3 %sums.1 = (f32[32,128]{1,0:T(8,128)S(1)}, f32[8,32]{1,0:T(8,128)S(1)}) custom-call(f32[32,128]{1,0:T(8,128)S(1)} %get-tuple-element.18.sums, f32[16,2176]{1,0:T(8,128)S(1)} %collective-permute-done.first1, f32[16,2176]{1,0:T(8,128)S(1)} %collective-permute-done.1.second1, f32[2,32,64]{2,1,0:T(8,128)S(1)} %copy-done.1, f32[8,128]{1,0:T(8,128)S(1)} %copy-done.5), custom_call_target="tpu_custom_call" | custom-call | tf_op jit(solution)/shard_map/sums/pallas_call | solution.py:337
  12.3 0.0 collective-permute-start.6
  12.3 1.5 %collective-permute-start.5 = (f32[8,32]{1,0:T(8,128)S(1)}, f32[8,32]{1,0:T(8,128)S(1)}, u32[]{:S(2)}, u32[]{:S(2)}) collective-permute-start(f32[8,32]{1,0:T(8,128)S(1)} %get-tuple-element.24.refs_0_), channel_id=1, source_target_pairs={{0,16},{8,24},{16,0},{24,8},{1,17},{9,25},{17,1},{25,9},{2,18},{10... | collective-permute-start | bytes 3080 | tf_op jit(solution)/shard_map/ppermute | solution.py:398
  13.9 0.2 %collective-permute-start.4 = (f32[8,32]{1,0:T(8,128)S(1)}, f32[8,32]{1,0:T(8,128)S(1)}, u32[]{:S(2)}, u32[]{:S(2)}) collective-permute-start(f32[8,32]{1,0:T(8,128)S(1)} %get-tuple-element.24.refs_0_), channel_id=1, source_target_pairs={{0,8},{8,16},{16,24},{24,0},{1,9},{9,17},{17,25},{25,1},{2,10},{10... | collective-permute-start | bytes 3080 | tf_op jit(solution)/shard_map/ppermute | solution.py:398
  14.1 0.0 copy-done
  14.1 0.0 copy-done.4
  14.1 0.7 %early.1 = (f32[32,4096]{1,0:T(8,128)S(1)}, f32[32,128]{1,0:T(8,128)S(1)}) custom-call(f32[32,4096]{1,0:T(8,128)S(1)} %get-tuple-element.15.live, f32[16,2176]{1,0:T(8,128)S(1)} %collective-permute-done.first1, f32[16,2176]{1,0:T(8,128)S(1)} %collective-permute-done.1.second1, f32[32,128]{1,0:T(8,128)S(1)} %get-tuple-element.19.sums, ...), custom_call_target="tpu_custom_call" | custom-call | tf_op jit(solution)/shard_map/early/pallas_call | solution.py:337
  14.8 1.1 %collective-permute-done.2.first2 = f32[16,2048]{1,0:T(8,128)S(1)} collective-permute-done((f32[16,2048]{1,0:T(8,128)S(1)}, f32[16,2048]{1,0:T(8,128)S(1)}, u32[]{:S(2)}, u32[]{:S(2)}) %collective-permute-start.2) | collective-permute-done | bytes 131104 | tf_op jit(solution)/shard_map/ppermute | solution.py:388
  15.9 0.0 collective-permute-done.3.second2
  15.9 0.0 collective-permute-done.6.refs_3_
  15.9 0.0 collective-permute-done.5.refs_2_
  16.0 0.9 %collective-permute-done.4.refs_1_ = f32[8,32]{1,0:T(8,128)S(1)} collective-permute-done((f32[8,32]{1,0:T(8,128)S(1)}, f32[8,32]{1,0:T(8,128)S(1)}, u32[]{:S(2)}, u32[]{:S(2)}) %collective-permute-start.4) | collective-permute-done | bytes 1056 | tf_op jit(solution)/shard_map/ppermute | solution.py:398
  16.9 0.0 copy-done.3
  16.9 1.7 %finish.1 = f32[32,4096]{1,0:T(8,128)} custom-call(f32[32,4096]{1,0:T(8,128)S(1)} %get-tuple-element.20.part, f32[32,128]{1,0:T(8,128)S(1)} %get-tuple-element.21.states, f32[16,2048]{1,0:T(8,128)S(1)} %collective-permute-done.2.first2, f32[16,2048]{1,0:T(8,128)S(1)} %collective-permute-done.3.second2, f32[2,32,64]{2,1,0:T(8,128)S(1)} %copy-done.1, ...), custom_call_target="tpu_custom_call" | custom-call | tf_op jit(solution)/shard_map/finish/pallas_call | solution.py:337
  (6 shorter events, 0.0 us)
Async XLA Ops:
  0.0 12.0 %copy-start.1 = (f32[2,32,64]{2,1,0:T(8,128)S(1)}, f32[2,32,64]{2,1,0:T(8,128)}, u32[]{:S(2)}) copy-start(f32[2,32,64]{2,1,0:T(8,128)} %constant.20.clone.mix) | copy-start | bytes 49156
  0.0 12.0 %copy-start.5 = (f32[8,128]{1,0:T(8,128)S(1)}, f32[8,128]{1,0:T(8,128)}, u32[]{:S(2)}) copy-start(f32[8,128]{1,0:T(8,128)} %constant.18.clone.whole) | copy-start | bytes 12292
  1.5 12.6 %copy-start = (bf16[512,256]{1,0:T(8,128)(2,1)S(1)}, bf16[512,256]{1,0:T(8,128)(2,1)}, u32[]{:S(2)}) copy-start(bf16[512,256]{1,0:T(8,128)(2,1)} %constant.15.clone.toeplitz) | copy-start | bytes 786436
  1.5 8.4 %collective-permute-start = (f32[16,2176]{1,0:T(8,128)S(1)}, f32[16,2176]{1,0:T(8,128)S(1)}, u32[]{:S(2)}, u32[]{:S(2)}) collective-permute-start(f32[16,2176]{1,0:T(8,128)S(1)} %get-tuple-element.16), channel_id=1, source_target_pairs={{0,1},{1,0},{2,3},{3,2},{4,5},{5,4},{6,7},{7,6},{8,9},{9,8},{10,11... | collective-permute-start | bytes 417800 | tf_op jit(solution)/shard_map/ppermute | solution.py:386
  3.1 9.0 %collective-permute-start.1 = (f32[16,2176]{1,0:T(8,128)S(1)}, f32[16,2176]{1,0:T(8,128)S(1)}, u32[]{:S(2)}, u32[]{:S(2)}) collective-permute-start(f32[16,2176]{1,0:T(8,128)S(1)} %get-tuple-element.17), channel_id=1, source_target_pairs={{1,2},{2,1},{3,4},{4,3},{5,6},{6,5},{9,10},{10,9},{11,12},{12,11},... | collective-permute-start | bytes 417800 | tf_op jit(solution)/shard_map/ppermute | solution.py:387
  5.4 10.5 %collective-permute-start.2 = (f32[16,2048]{1,0:T(8,128)S(1)}, f32[16,2048]{1,0:T(8,128)S(1)}, u32[]{:S(2)}, u32[]{:S(2)}) collective-permute-start(f32[16,2048]{1,0:T(8,128)S(1)} %get-tuple-element.22), channel_id=1, source_target_pairs={{0,1},{1,0},{2,3},{3,2},{4,5},{5,4},{6,7},{7,6},{8,9},{9,8},{10,11... | collective-permute-start | bytes 393224 | tf_op jit(solution)/shard_map/ppermute | solution.py:388
  5.5 10.5 %collective-permute-start.3 = (f32[16,2048]{1,0:T(8,128)S(1)}, f32[16,2048]{1,0:T(8,128)S(1)}, u32[]{:S(2)}, u32[]{:S(2)}) collective-permute-start(f32[16,2048]{1,0:T(8,128)S(1)} %get-tuple-element.23), channel_id=1, source_target_pairs={{1,2},{2,1},{3,4},{4,3},{5,6},{6,5},{9,10},{10,9},{11,12},{12,11},... | collective-permute-start | bytes 393224 | tf_op jit(solution)/shard_map/ppermute | solution.py:389
  12.0 2.1 %copy-start.4 = (f32[128,128]{1,0:T(8,128)S(1)}, f32[128,128]{1,0:T(8,128)}, u32[]{:S(2)}) copy-start(f32[128,128]{1,0:T(8,128)} %constant.17.clone.inner) | copy-start | bytes 196612
  12.3 3.6 %collective-permute-start.6 = (f32[8,32]{1,0:T(8,128)S(1)}, f32[8,32]{1,0:T(8,128)S(1)}, u32[]{:S(2)}, u32[]{:S(2)}) collective-permute-start(f32[8,32]{1,0:T(8,128)S(1)} %get-tuple-element.24.refs_0_), channel_id=1, source_target_pairs={{0,24},{8,0},{16,8},{24,16},{1,25},{9,1},{17,9},{25,17},{2,26},{10... | collective-permute-start | bytes 3080 | tf_op jit(solution)/shard_map/ppermute | solution.py:398
  12.3 3.6 %collective-permute-start.5 = (f32[8,32]{1,0:T(8,128)S(1)}, f32[8,32]{1,0:T(8,128)S(1)}, u32[]{:S(2)}, u32[]{:S(2)}) collective-permute-start(f32[8,32]{1,0:T(8,128)S(1)} %get-tuple-element.24.refs_0_), channel_id=1, source_target_pairs={{0,16},{8,24},{16,0},{24,8},{1,17},{9,25},{17,1},{25,9},{2,18},{10... | collective-permute-start | bytes 3080 | tf_op jit(solution)/shard_map/ppermute | solution.py:398
  13.9 3.0 %collective-permute-start.4 = (f32[8,32]{1,0:T(8,128)S(1)}, f32[8,32]{1,0:T(8,128)S(1)}, u32[]{:S(2)}, u32[]{:S(2)}) collective-permute-start(f32[8,32]{1,0:T(8,128)S(1)} %get-tuple-element.24.refs_0_), channel_id=1, source_target_pairs={{0,8},{8,16},{16,24},{24,0},{1,9},{9,17},{17,25},{25,1},{2,10},{10... | collective-permute-start | bytes 3080 | tf_op jit(solution)/shard_map/ppermute | solution.py:398
  14.1 2.8 %copy-start.2 = (bf16[256,256]{1,0:T(8,128)(2,1)S(1)}, bf16[256,256]{1,0:T(8,128)(2,1)}, u32[]{:S(2)}) copy-start(bf16[256,256]{1,0:T(8,128)(2,1)} %constant.16.clone.spread) | copy-start | bytes 393220
  14.1 2.8 %copy-start.3 = (f32[4,32,128]{2,1,0:T(8,128)S(1)}, f32[4,32,128]{2,1,0:T(8,128)}, u32[]{:S(2)}) copy-start(f32[4,32,128]{2,1,0:T(8,128)} %constant.19.clone.enter) | copy-start | bytes 196612

commit v3 on v2

--- a/solution.py
+++ b/solution.py
@@ -12,7 +12,7 @@
 RADIUS = 16
 BLOCK = 256
 STATES = 8
-SUMS_COST = 0
+SUMS_COST = 6
 
 low_corner = 0.015
 high_corner = 100.0
@@ -90,6 +90,12 @@
     for i, p in enumerate(poles**steps):
         out[2 * i : 2 * i + 2, 2 * i : 2 * i + 2] = [[p.real, -p.imag], [p.imag, p.real]]
     return out
+
+
+def met(place, step, parts):
+    if parts & (parts - 1) == 0:
+        return place ^ step, place ^ step
+    return (place + step) % parts, (place - step) % parts
 
 
 def time_tables(samples, parts):
@@ -132,7 +138,7 @@
     enter = np.zeros((parts, parts * STATES, lanes))
     for t in range(parts):
         for j in range(parts):
-            at = (t - j) % parts
+            at = met(t, j, parts)[1]
             into = np.zeros((STATES, STATES))
             if at < t:
                 into[:4, :4] = device[t - at - 1]
@@ -207,15 +213,16 @@
     )
 
 
-def spreading(states, first, groups, spread):
+def spreading(states, groups, spread):
     lanes = states.shape[1]
     owner = lax.broadcasted_iota(jnp.int32, states.shape, 1) // STATES
-    rows = [jnp.where(owner == first + g, states, 0.0) for g in range(groups)]
-    high, low = split(jnp.concatenate(rows, axis=0))
+    high, low = split(
+        jnp.concatenate([jnp.where(owner == g, states, 0.0) for g in range(groups)], axis=0)
+    )
     above, below = spread[:lanes], spread[lanes:]
     return product(
-        jnp.concatenate([high, low], axis=1), jnp.concatenate([above, above], axis=0)
-    ) + product(high, below)
+        jnp.concatenate([high, low, high], axis=1), jnp.concatenate([above, above, below], axis=0)
+    )
 
 
 def start_kernel(cuts, x_hbm, mask_hbm, gather_hbm, *refs):
@@ -292,32 +299,49 @@
         out[:, b * BLOCK : (b + 1) * BLOCK] = rows[b * channels : (b + 1) * channels]
 
 
-def finish_kernel(cuts, part, states, first2, second2, mix, toeplitz, enter, spread, *refs):
-    devices, (out_hbm, out, sems) = refs[:-3], refs[-3:]
+def edge_rows(which, edge, mix, toeplitz, channels):
+    at = channels + which * RADIUS
+    weights = mix[place()][:, at : at + RADIUS]
+    return filtering(rows_of(mixing(weights, edge)), toeplitz[...])
+
+
+def late_kernel(part, second2, mix, toeplitz, out):
     channels, samples = part.shape
-    cut = min(cuts)
-    at = lax.axis_index("tm")
+    start = samples - second2.shape[1]
+    rows = edge_rows(1, second2[...], mix, toeplitz, channels)
+    out[:, :start] = part[:, :start]
+    for b in range((samples - start) // BLOCK):
+        here = slice(start + b * BLOCK, start + (b + 1) * BLOCK)
+        out[:, here] = part[:, here] + rows[b * channels : (b + 1) * channels]
+
+
+def enter_kernel(part, states, enter, spread, *refs):
+    devices, out = refs[:-1], refs[-1]
+    channels, samples = part.shape
     arrived = jnp.concatenate([ref[...] for ref in devices], axis=0)
     inside = states[...] + lax.dot_general(
-        arrived, enter[at], (((0,), (0,)), ((), ())), precision=highest
-    )
-    weights = mix[place()][:, channels:]
-    stores = []
-    for i, (start, stop) in enumerate(((0, cut), (cut, samples))):
-        groups = (stop - start) // BLOCK
-        rows = spreading(inside, start // BLOCK, groups, spread[...])
-        if i == 1:
-            edges = [padded(ref[...], stop - start - ref.shape[1], 0) for ref in (first2, second2)]
-            mixed = mixing(weights, jnp.concatenate(edges, axis=0))
-            rows += filtering(rows_of(mixed), toeplitz[...])
-        for b in range(groups):
-            here = slice(start + b * BLOCK, start + (b + 1) * BLOCK)
-            out[:, here] = part[:, here] + rows[b * channels : (b + 1) * channels]
-        p = pl.ds(start, stop - start)
-        stores.append(pltpu.make_async_copy(out.at[:, p], out_hbm.at[:, p], sems.at[i]))
-        stores[-1].start()
-    for copy in stores:
-        copy.wait()
+        arrived, enter[lax.axis_index("tm")], (((0,), (0,)), ((), ())), precision=highest
+    )
+    groups = samples // BLOCK
+    rows = spreading(inside, groups, spread[...])
+    for b in range(groups):
+        here = slice(b * BLOCK, (b + 1) * BLOCK)
+        out[:, here] = part[:, here] + rows[b * channels : (b + 1) * channels]
+
+
+def finish_kernel(part, first2, mix, toeplitz, out_hbm, out, sems):
+    channels, samples = part.shape
+    start = samples - first2.shape[1]
+    done = pltpu.make_async_copy(part.at[:, :start], out_hbm.at[:, :start], sems.at[0])
+    done.start()
+    rows = edge_rows(0, first2[...], mix, toeplitz, channels)
+    for b in range((samples - start) // BLOCK):
+        here = slice(start + b * BLOCK, start + (b + 1) * BLOCK)
+        out[:, b * BLOCK : (b + 1) * BLOCK] = part[:, here] + rows[b * channels : (b + 1) * channels]
+    last = pltpu.make_async_copy(out, out_hbm.at[:, start:], sems.at[1])
+    last.start()
+    done.wait()
+    last.wait()
 
 
 def vmem(*shape, dtype=jnp.float32):
@@ -341,7 +365,7 @@
         out_specs=out_specs[0] if single else tuple(out_specs),
         scratch_shapes=list(scratch),
         compiler_params=pltpu.CompilerParams(vmem_limit_bytes=24 * 1024 * 1024),
-        cost_estimate=pl.CostEstimate(flops=cost * 1000000000, bytes_accessed=0, transcendentals=0),
+        cost_estimate=pl.CostEstimate(flops=cost * 100000000, bytes_accessed=0, transcendentals=0),
         name=name,
     )(*inputs)
 
@@ -351,7 +375,7 @@
     parts = lax.axis_size("tm")
     places = lax.axis_size("chan")
     lanes = samples // BLOCK * STATES
-    cuts = (samples // 2, samples // 2)
+    cuts = (samples * 5 // 8 // BLOCK * BLOCK, samples * 3 // 8 // BLOCK * BLOCK)
     toeplitz, gather, spread, inner, whole, enter = time_tables(samples, parts)
     gather = jnp.asarray(np.concatenate(halves(gather), axis=1))
     toeplitz = jnp.asarray(np.concatenate(halves(toeplitz), axis=0))
@@ -395,7 +419,7 @@
         cost=SUMS_COST,
     )
     others = [
-        lax.ppermute(device, "tm", [(i, (i + j) % parts) for i in range(parts)])
+        lax.ppermute(device, "tm", [(i, met(i, j, parts)[0]) for i in range(parts)])
         for j in range(1, parts)
     ]
     part, states = kernel(
@@ -404,12 +428,19 @@
         [live, first1, second1, sums, mix, toeplitz, inner],
         [vmem(channels, samples), vmem(channels, lanes)],
     )
+    part = kernel(late_kernel, "late", [part, second2, mix, toeplitz], [vmem(channels, samples)])
+    part = kernel(
+        enter_kernel,
+        "enter",
+        [part, states, enter, spread, device, *others],
+        [vmem(channels, samples)],
+    )
     return kernel(
-        functools.partial(finish_kernel, cuts),
+        finish_kernel,
         "finish",
-        [part, states, first2, second2, mix, toeplitz, enter, spread, device, *others],
+        [part, first2, mix, toeplitz],
         [jax.ShapeDtypeStruct((channels, samples), jnp.float32)],
-        [vmem(channels, samples), pltpu.SemaphoreType.DMA((2,))],
+        [vmem(channels, samples - cuts[0]), pltpu.SemaphoreType.DMA((2,))],
     )
 
 

time: 18.7 us -> 17.8 us (0.952)
  the two profiles are of different devices: /device:TPU:24 before, /device:TPU:0 now
where the time goes in v3:
time: 17.8 us; the launch traced here: 17.6 us
  starting transfers between devices  12 us (67%)
  Pallas kernels  4.55 us (26%)
  waiting for transfers between devices  0.84 us (5%)
    ppermute x1, starting transfers between devices, shards(): first2 = lax.ppermute(first2, 'chan', pairs[0])  5.59 us
    pallas_call x6, Pallas kernels, kernel(): pl.pallas_call(body, out_shape=outputs[0] if single else tuple(outputs),...  4.55 us
    ppermute x1, starting transfers between devices, shards(): first1 = lax.ppermute(first1, 'chan', pairs[0])  3 us
    ppermute x3, starting transfers between devices, shards(): lax.ppermute(device, 'tm', [(i, met(i, j, parts)[0]) for i in range(parts)])  2.07 us
    ppermute x1, starting transfers between devices, shards(): second2 = lax.ppermute(second2, 'chan', pairs[1])  0.67 us
    ppermute x1, starting transfers between devices, shards(): second1 = lax.ppermute(second1, 'chan', pairs[1])  0.66 us
    ppermute x3, waiting for transfers between devices, shards(): lax.ppermute(device, 'tm', [(i, met(i, j, parts)[0]) for i in range(parts)])  0.59 us
  transfers between devices with their start and end apart: 7, of which 2 were waited for; matrix products, arithmetic and copies ran while one was open for 0% of the time, Pallas kernels for 11%

profile of v3, /device:TPU:0, one launch (start us, length us, event | category | flops | bytes accessed | tf_op | source)
XLA Modules:
  0.0 17.6 jit_solution(8482193072914439770)
XLA Ops:
  0.0 1.5 %start.1 = (f32[16,2688]{1,0:T(8,128)S(1)}, f32[16,1664]{1,0:T(8,128)S(1)}, f32[16,1536]{1,0:T(8,128)S(1)}, f32[16,2560]{1,0:T(8,128)S(1)}, f32[32,4096]{1,0:T(8,128)S(1)}, /*index=5*/f32[32,128]{1,0:T(8,128)S(1)}) custom-call(f32[32,4096]{1,0:T(8,128)} %x_hbm.1, s32[1,32]{1,0:T(1,128)} %bitcast.1, bf16[256,256]{1,0:T(8,128)(2,1)} %constant.14.clone.gather_hbm), custom_call_target="tpu_custom_call" | custom-call | tf_op jit(solution)/shard_map/start/pallas_call | solution.py:361
  1.5 0.0 copy-start.5
  1.5 3.0 %collective-permute-start = (f32[16,2688]{1,0:T(8,128)S(1)}, f32[16,2688]{1,0:T(8,128)S(1)}, u32[]{:S(2)}, u32[]{:S(2)}) collective-permute-start(f32[16,2688]{1,0:T(8,128)S(1)} %get-tuple-element.16), channel_id=1, source_target_pairs={{0,1},{1,0},{2,3},{3,2},{4,5},{5,4},{6,7},{7,6},{8,9},{9,8},{10,11... | collective-permute-start | bytes 516104 | tf_op jit(solution)/shard_map/ppermute | solution.py:410
  4.5 0.7 %collective-permute-start.1 = (f32[16,1664]{1,0:T(8,128)S(1)}, f32[16,1664]{1,0:T(8,128)S(1)}, u32[]{:S(2)}, u32[]{:S(2)}) collective-permute-start(f32[16,1664]{1,0:T(8,128)S(1)} %get-tuple-element.17), channel_id=1, source_target_pairs={{1,2},{2,1},{3,4},{4,3},{5,6},{6,5},{9,10},{10,9},{11,12},{12,11},... | collective-permute-start | bytes 319496 | tf_op jit(solution)/shard_map/ppermute | solution.py:411
  5.2 0.7 %collective-permute-start.2 = (f32[16,2560]{1,0:T(8,128)S(1)}, f32[16,2560]{1,0:T(8,128)S(1)}, u32[]{:S(2)}, u32[]{:S(2)}) collective-permute-start(f32[16,2560]{1,0:T(8,128)S(1)} %get-tuple-element.21), channel_id=1, source_target_pairs={{1,2},{2,1},{3,4},{4,3},{5,6},{6,5},{9,10},{10,9},{11,12},{12,11},... | collective-permute-start | bytes 491528 | tf_op jit(solution)/shard_map/ppermute | solution.py:413
  5.8 5.6 %collective-permute-start.6 = (f32[16,1536]{1,0:T(8,128)S(1)}, f32[16,1536]{1,0:T(8,128)S(1)}, u32[]{:S(2)}, u32[]{:S(2)}) collective-permute-start(f32[16,1536]{1,0:T(8,128)S(1)} %get-tuple-element.24), channel_id=1, source_target_pairs={{0,1},{1,0},{2,3},{3,2},{4,5},{5,4},{6,7},{7,6},{8,9},{9,8},{10,11... | collective-permute-start | bytes 294920 | tf_op jit(solution)/shard_map/ppermute | solution.py:412
  11.4 0.0 collective-permute-done.1.second1
  11.4 0.0 collective-permute-done.first1
  11.5 0.0 copy-start
  11.5 0.0 copy-start.4
  11.5 0.3 %sums.1 = (f32[32,128]{1,0:T(8,128)S(1)}, f32[8,32]{1,0:T(8,128)S(1)}) custom-call(f32[32,128]{1,0:T(8,128)S(1)} %get-tuple-element.18.sums, f32[16,2688]{1,0:T(8,128)S(1)} %collective-permute-done.first1, f32[16,1664]{1,0:T(8,128)S(1)} %collective-permute-done.1.second1, f32[2,32,64]{2,1,0:T(8,128)S(1)} %copy-done.1, f32[8,128]{1,0:T(8,128)S(1)} %copy-done.5), custom_call_target="tpu_custom_call" | custom-call | flops 600000000 | tf_op jit(solution)/shard_map/sums/pallas_call | solution.py:361
  11.8 0.3 %collective-permute-start.5 = (f32[8,32]{1,0:T(8,128)S(1)}, f32[8,32]{1,0:T(8,128)S(1)}, u32[]{:S(2)}, u32[]{:S(2)}) collective-permute-start(f32[8,32]{1,0:T(8,128)S(1)} %get-tuple-element.23.refs_0_), channel_id=1, source_target_pairs={{0,24},{8,16},{16,8},{24,0},{1,25},{9,17},{17,9},{25,1},{2,26},{10... | collective-permute-start | bytes 3080 | tf_op jit(solution)/shard_map/ppermute | solution.py:422
  12.1 1.7 %collective-permute-start.4 = (f32[8,32]{1,0:T(8,128)S(1)}, f32[8,32]{1,0:T(8,128)S(1)}, u32[]{:S(2)}, u32[]{:S(2)}) collective-permute-start(f32[8,32]{1,0:T(8,128)S(1)} %get-tuple-element.23.refs_0_), channel_id=1, source_target_pairs={{0,16},{8,24},{16,0},{24,8},{1,17},{9,25},{17,1},{25,9},{2,18},{10... | collective-permute-start | bytes 3080 | tf_op jit(solution)/shard_map/ppermute | solution.py:422
  13.8 0.1 collective-permute-start.3
  13.9 0.7 %early.1 = (f32[32,4096]{1,0:T(8,128)S(1)}, f32[32,128]{1,0:T(8,128)S(1)}) custom-call(f32[32,4096]{1,0:T(8,128)S(1)} %get-tuple-element.15.live, f32[16,2688]{1,0:T(8,128)S(1)} %collective-permute-done.first1, f32[16,1664]{1,0:T(8,128)S(1)} %collective-permute-done.1.second1, f32[32,128]{1,0:T(8,128)S(1)} %get-tuple-element.19.sums, ...), custom_call_target="tpu_custom_call" | custom-call | tf_op jit(solution)/shard_map/early/pallas_call | solution.py:361
  14.6 0.0 collective-permute-done.2.second2
  14.6 0.0 copy-start.2
  14.6 0.0 copy-start.3
  14.6 0.5 %late.1.part = f32[32,4096]{1,0:T(8,128)S(1)} custom-call(f32[32,4096]{1,0:T(8,128)S(1)} %get-tuple-element.20.part, f32[16,2560]{1,0:T(8,128)S(1)} %collective-permute-done.2.second2, f32[2,32,64]{2,1,0:T(8,128)S(1)} %copy-done.1, bf16[512,256]{1,0:T(8,128)(2,1)S(1)} %copy-done), custom_call_target="tpu_custom_call" | custom-call | tf_op jit(solution)/shard_map/late/pallas_call | solution.py:361
  15.1 0.0 collective-permute-done.5.refs_3_
  15.1 0.6 %collective-permute-done.4.refs_2_ = f32[8,32]{1,0:T(8,128)S(1)} collective-permute-done((f32[8,32]{1,0:T(8,128)S(1)}, f32[8,32]{1,0:T(8,128)S(1)}, u32[]{:S(2)}, u32[]{:S(2)}) %collective-permute-start.4) | collective-permute-done | bytes 1056 | tf_op jit(solution)/shard_map/ppermute | solution.py:422
  15.7 0.5 %enter.2.part = f32[32,4096]{1,0:T(8,128)S(1)} custom-call(f32[32,4096]{1,0:T(8,128)S(1)} %late.1.part, f32[32,128]{1,0:T(8,128)S(1)} %get-tuple-element.22.states, f32[4,32,128]{2,1,0:T(8,128)S(1)} %copy-done.3, bf16[256,256]{1,0:T(8,128)(2,1)S(1)} %copy-done.2, f32[8,32]{1,0:T(8,128)S(1)} %get-tuple-element.23.refs_0_, ...), custom_call_target="tpu_custom_call" | custom-call | tf_op jit(solution)/shard_map/enter/pallas_call | solution.py:361
  16.2 0.2 %collective-permute-done.6.first2 = f32[16,1536]{1,0:T(8,128)S(1)} collective-permute-done((f32[16,1536]{1,0:T(8,128)S(1)}, f32[16,1536]{1,0:T(8,128)S(1)}, u32[]{:S(2)}, u32[]{:S(2)}) %collective-permute-start.6) | collective-permute-done | bytes 98336 | tf_op jit(solution)/shard_map/ppermute | solution.py:412
  16.4 1.1 %finish.1 = f32[32,4096]{1,0:T(8,128)} custom-call(f32[32,4096]{1,0:T(8,128)S(1)} %enter.2.part, f32[16,1536]{1,0:T(8,128)S(1)} %collective-permute-done.6.first2, f32[2,32,64]{2,1,0:T(8,128)S(1)} %copy-done.1, bf16[512,256]{1,0:T(8,128)(2,1)S(1)} %copy-done), custom_call_target="tpu_custom_call" | custom-call | tf_op jit(solution)/shard_map/finish/pallas_call | solution.py:361
  (8 shorter events, 0.0 us)
Async XLA Ops:
  0.0 11.4 %copy-start.1 = (f32[2,32,64]{2,1,0:T(8,128)S(1)}, f32[2,32,64]{2,1,0:T(8,128)}, u32[]{:S(2)}) copy-start(f32[2,32,64]{2,1,0:T(8,128)} %constant.20.clone.mix) | copy-start | bytes 49156
  1.5 10.0 %copy-start.5 = (f32[8,128]{1,0:T(8,128)S(1)}, f32[8,128]{1,0:T(8,128)}, u32[]{:S(2)}) copy-start(f32[8,128]{1,0:T(8,128)} %constant.18.clone.whole) | copy-start | bytes 12292
  1.5 9.9 %collective-permute-start = (f32[16,2688]{1,0:T(8,128)S(1)}, f32[16,2688]{1,0:T(8,128)S(1)}, u32[]{:S(2)}, u32[]{:S(2)}) collective-permute-start(f32[16,2688]{1,0:T(8,128)S(1)} %get-tuple-element.16), channel_id=1, source_target_pairs={{0,1},{1,0},{2,3},{3,2},{4,5},{5,4},{6,7},{7,6},{8,9},{9,8},{10,11... | collective-permute-start | bytes 516104 | tf_op jit(solution)/shard_map/ppermute | solution.py:410
  4.5 6.9 %collective-permute-start.1 = (f32[16,1664]{1,0:T(8,128)S(1)}, f32[16,1664]{1,0:T(8,128)S(1)}, u32[]{:S(2)}, u32[]{:S(2)}) collective-permute-start(f32[16,1664]{1,0:T(8,128)S(1)} %get-tuple-element.17), channel_id=1, source_target_pairs={{1,2},{2,1},{3,4},{4,3},{5,6},{6,5},{9,10},{10,9},{11,12},{12,11},... | collective-permute-start | bytes 319496 | tf_op jit(solution)/shard_map/ppermute | solution.py:411
  5.2 9.4 %collective-permute-start.2 = (f32[16,2560]{1,0:T(8,128)S(1)}, f32[16,2560]{1,0:T(8,128)S(1)}, u32[]{:S(2)}, u32[]{:S(2)}) collective-permute-start(f32[16,2560]{1,0:T(8,128)S(1)} %get-tuple-element.21), channel_id=1, source_target_pairs={{1,2},{2,1},{3,4},{4,3},{5,6},{6,5},{9,10},{10,9},{11,12},{12,11},... | collective-permute-start | bytes 491528 | tf_op jit(solution)/shard_map/ppermute | solution.py:413
  5.8 10.6 %collective-permute-start.6 = (f32[16,1536]{1,0:T(8,128)S(1)}, f32[16,1536]{1,0:T(8,128)S(1)}, u32[]{:S(2)}, u32[]{:S(2)}) collective-permute-start(f32[16,1536]{1,0:T(8,128)S(1)} %get-tuple-element.24), channel_id=1, source_target_pairs={{0,1},{1,0},{2,3},{3,2},{4,5},{5,4},{6,7},{7,6},{8,9},{9,8},{10,11... | collective-permute-start | bytes 294920 | tf_op jit(solution)/shard_map/ppermute | solution.py:412
  11.5 2.4 %copy-start = (bf16[512,256]{1,0:T(8,128)(2,1)S(1)}, bf16[512,256]{1,0:T(8,128)(2,1)}, u32[]{:S(2)}) copy-start(bf16[512,256]{1,0:T(8,128)(2,1)} %constant.15.clone.toeplitz) | copy-start | bytes 786436
  11.5 2.4 %copy-start.4 = (f32[128,128]{1,0:T(8,128)S(1)}, f32[128,128]{1,0:T(8,128)}, u32[]{:S(2)}) copy-start(f32[128,128]{1,0:T(8,128)} %constant.17.clone.inner) | copy-start | bytes 196612
  11.8 3.3 %collective-permute-start.5 = (f32[8,32]{1,0:T(8,128)S(1)}, f32[8,32]{1,0:T(8,128)S(1)}, u32[]{:S(2)}, u32[]{:S(2)}) collective-permute-start(f32[8,32]{1,0:T(8,128)S(1)} %get-tuple-element.23.refs_0_), channel_id=1, source_target_pairs={{0,24},{8,16},{16,8},{24,0},{1,25},{9,17},{17,9},{25,1},{2,26},{10... | collective-permute-start | bytes 3080 | tf_op jit(solution)/shard_map/ppermute | solution.py:422
  12.1 3.6 %collective-permute-start.4 = (f32[8,32]{1,0:T(8,128)S(1)}, f32[8,32]{1,0:T(8,128)S(1)}, u32[]{:S(2)}, u32[]{:S(2)}) collective-permute-start(f32[8,32]{1,0:T(8,128)S(1)} %get-tuple-element.23.refs_0_), channel_id=1, source_target_pairs={{0,16},{8,24},{16,0},{24,8},{1,17},{9,25},{17,1},{25,9},{2,18},{10... | collective-permute-start | bytes 3080 | tf_op jit(solution)/shard_map/ppermute | solution.py:422
  13.8 1.9 %collective-permute-start.3 = (f32[8,32]{1,0:T(8,128)S(1)}, f32[8,32]{1,0:T(8,128)S(1)}, u32[]{:S(2)}, u32[]{:S(2)}) collective-permute-start(f32[8,32]{1,0:T(8,128)S(1)} %get-tuple-element.23.refs_0_), channel_id=1, source_target_pairs={{0,8},{8,0},{16,24},{24,16},{1,9},{9,1},{17,25},{25,17},{2,10},{10... | collective-permute-start | bytes 3080 | tf_op jit(solution)/shard_map/ppermute | solution.py:422
  14.6 1.1 %copy-start.2 = (bf16[256,256]{1,0:T(8,128)(2,1)S(1)}, bf16[256,256]{1,0:T(8,128)(2,1)}, u32[]{:S(2)}) copy-start(bf16[256,256]{1,0:T(8,128)(2,1)} %constant.16.clone.spread) | copy-start | bytes 393220
  14.6 1.1 %copy-start.3 = (f32[4,32,128]{2,1,0:T(8,128)S(1)}, f32[4,32,128]{2,1,0:T(8,128)}, u32[]{:S(2)}) copy-start(f32[4,32,128]{2,1,0:T(8,128)} %constant.19.clone.enter) | copy-start | bytes 196612

commit v4 on v3

--- a/solution.py
+++ b/solution.py
@@ -12,7 +12,7 @@
 RADIUS = 16
 BLOCK = 256
 STATES = 8
-SUMS_COST = 6
+SUMS_COST = 10
 
 low_corner = 0.015
 high_corner = 100.0
@@ -213,11 +213,22 @@
     )
 
 
-def spreading(states, groups, spread):
+def turned(a, b):
+    a_high, a_low = split(a)
+    b_high, b_low = split(b)
+    return lax.dot_general(
+        jnp.concatenate([a_high, a_low, a_high], axis=0),
+        jnp.concatenate([b_high, b_high, b_low], axis=0),
+        (((0,), (0,)), ((), ())),
+        preferred_element_type=jnp.float32,
+    )
+
+
+def spreading(states, first, groups, spread):
     lanes = states.shape[1]
     owner = lax.broadcasted_iota(jnp.int32, states.shape, 1) // STATES
     high, low = split(
-        jnp.concatenate([jnp.where(owner == g, states, 0.0) for g in range(groups)], axis=0)
+        jnp.concatenate([jnp.where(owner == first + g, states, 0.0) for g in range(groups)], axis=0)
     )
     above, below = spread[:lanes], spread[lanes:]
     return product(
@@ -288,15 +299,24 @@
     return jnp.concatenate([v for v in (sides[0], value, sides[1]) if v is not None], axis=1)
 
 
-def early_kernel(live, first1, second1, sums, mix, toeplitz, inner, out, states):
+def early_kernel(live, first1, second1, sums, mix, toeplitz, inner, enter_hbm, spread_hbm, *refs):
+    out, states, enter, spread, sems = refs
     channels, samples = live.shape
     lanes = sums.shape[1]
+    copies = [
+        pltpu.make_async_copy(enter_hbm.at[lax.axis_index("tm")], enter, sems.at[0]),
+        pltpu.make_async_copy(spread_hbm, spread, sems.at[1]),
+    ]
+    for copy in copies:
+        copy.start()
     states[...] = exact(sums[...], inner[...])
     edges = [padded(ref[:, lanes:], 0, samples + lanes - ref.shape[1]) for ref in (first1, second1)]
     mixed = mixing(mix[place()], jnp.concatenate([live[...], *edges], axis=0))
     rows = filtering(rows_of(mixed), toeplitz[...])
     for b in range(samples // BLOCK):
         out[:, b * BLOCK : (b + 1) * BLOCK] = rows[b * channels : (b + 1) * channels]
+    for copy in copies:
+        copy.wait()
 
 
 def edge_rows(which, edge, mix, toeplitz, channels):
@@ -315,33 +335,27 @@
         out[:, here] = part[:, here] + rows[b * channels : (b + 1) * channels]
 
 
-def enter_kernel(part, states, enter, spread, *refs):
-    devices, out = refs[:-1], refs[-1]
-    channels, samples = part.shape
-    arrived = jnp.concatenate([ref[...] for ref in devices], axis=0)
-    inside = states[...] + lax.dot_general(
-        arrived, enter[lax.axis_index("tm")], (((0,), (0,)), ((), ())), precision=highest
-    )
-    groups = samples // BLOCK
-    rows = spreading(inside, groups, spread[...])
-    for b in range(groups):
-        here = slice(b * BLOCK, (b + 1) * BLOCK)
-        out[:, here] = part[:, here] + rows[b * channels : (b + 1) * channels]
-
-
-def finish_kernel(part, first2, mix, toeplitz, out_hbm, out, sems):
+def finish_kernel(pieces, part, states, first2, mix, toeplitz, enter, spread, *refs):
+    devices, (out_hbm, out, sems) = refs[:-3], refs[-3:]
     channels, samples = part.shape
     start = samples - first2.shape[1]
-    done = pltpu.make_async_copy(part.at[:, :start], out_hbm.at[:, :start], sems.at[0])
-    done.start()
-    rows = edge_rows(0, first2[...], mix, toeplitz, channels)
-    for b in range((samples - start) // BLOCK):
-        here = slice(start + b * BLOCK, start + (b + 1) * BLOCK)
-        out[:, b * BLOCK : (b + 1) * BLOCK] = part[:, here] + rows[b * channels : (b + 1) * channels]
-    last = pltpu.make_async_copy(out, out_hbm.at[:, start:], sems.at[1])
-    last.start()
-    done.wait()
-    last.wait()
+    arrived = jnp.concatenate([ref[...] for ref in devices], axis=0)
+    inside = states[...] + turned(arrived, enter[...])
+    stores = []
+    for i, (low, high) in enumerate(pieces):
+        groups = (high - low) // BLOCK
+        rows = spreading(inside, low // BLOCK, groups, spread[...])
+        if low >= start:
+            edge = first2[:, low - start : high - start]
+            rows += edge_rows(0, edge, mix, toeplitz, channels)
+        for b in range(groups):
+            here = slice(low + b * BLOCK, low + (b + 1) * BLOCK)
+            out[:, here] = part[:, here] + rows[b * channels : (b + 1) * channels]
+        p = pl.ds(low, high - low)
+        stores.append(pltpu.make_async_copy(out.at[:, p], out_hbm.at[:, p], sems.at[i]))
+        stores[-1].start()
+    for copy in stores:
+        copy.wait()
 
 
 def vmem(*shape, dtype=jnp.float32):
@@ -375,7 +389,7 @@
     parts = lax.axis_size("tm")
     places = lax.axis_size("chan")
     lanes = samples // BLOCK * STATES
-    cuts = (samples * 5 // 8 // BLOCK * BLOCK, samples * 3 // 8 // BLOCK * BLOCK)
+    cuts = (samples * 3 // 4 // BLOCK * BLOCK, samples * 5 // 16 // BLOCK * BLOCK)
     toeplitz, gather, spread, inner, whole, enter = time_tables(samples, parts)
     gather = jnp.asarray(np.concatenate(halves(gather), axis=1))
     toeplitz = jnp.asarray(np.concatenate(halves(toeplitz), axis=0))
@@ -422,25 +436,29 @@
         lax.ppermute(device, "tm", [(i, met(i, j, parts)[0]) for i in range(parts)])
         for j in range(1, parts)
     ]
-    part, states = kernel(
+    part, states, enter, spread = kernel(
         early_kernel,
         "early",
-        [live, first1, second1, sums, mix, toeplitz, inner],
-        [vmem(channels, samples), vmem(channels, lanes)],
+        [live, first1, second1, sums, mix, toeplitz, inner, enter, spread],
+        [
+            vmem(channels, samples),
+            vmem(channels, lanes),
+            vmem(*enter.shape[1:]),
+            vmem(*spread.shape, dtype=jnp.bfloat16),
+        ],
+        [pltpu.SemaphoreType.DMA((2,))],
+        far=(7, 8),
     )
     part = kernel(late_kernel, "late", [part, second2, mix, toeplitz], [vmem(channels, samples)])
-    part = kernel(
-        enter_kernel,
-        "enter",
-        [part, states, enter, spread, device, *others],
-        [vmem(channels, samples)],
-    )
+    step = max(BLOCK, samples // 4 // BLOCK * BLOCK)
+    edges = sorted({cuts[0], samples, *range(0, samples, step)})
+    pieces = list(zip(edges[:-1], edges[1:]))[::-1]
     return kernel(
-        finish_kernel,
+        functools.partial(finish_kernel, pieces),
         "finish",
-        [part, first2, mix, toeplitz],
+        [part, states, first2, mix, toeplitz, enter, spread, device, *others],
         [jax.ShapeDtypeStruct((channels, samples), jnp.float32)],
-        [vmem(channels, samples - cuts[0]), pltpu.SemaphoreType.DMA((2,))],
+        [vmem(channels, samples), pltpu.SemaphoreType.DMA((len(pieces),))],
     )
 
 

time: 17.8 us -> 17.8 us (level)
  Pallas kernels: 4.55 us -> 4.79 us
  waiting for transfers between devices: 0.84 us -> 0.65 us
    ppermute x3, waiting for transfers between devices: 0.59 us -> 0.01 us  [shards(): lax.ppermute(device, 'tm', [(i, met(i, j, parts)[0]) for i in range(parts)])]
    ppermute x1, waiting for transfers between devices: 0.24 us -> 0.64 us  [shards(): first2 = lax.ppermute(first2, 'chan', pairs[0])]
    pallas_call x6 -> x5, Pallas kernels: 4.55 us -> 4.79 us  [kernel(): pl.pallas_call(body, out_shape=outputs[0] if single else tuple(outputs),...]
  transfers between devices with their start and end apart: 7 -> 7, of which waited for: 2 -> 1; matrix products, arithmetic and copies ran while one was open for 0% -> 0% of each run, Pallas kernels for 11% -> 11%
where the time goes in v4:
time: 17.8 us; the launch traced here: 17.6 us
  starting transfers between devices  12 us (67%)
  Pallas kernels  4.79 us (27%)
  waiting for transfers between devices  0.65 us (4%)
    ppermute x1, starting transfers between devices, shards(): first2 = lax.ppermute(first2, 'chan', pairs[0])  5.59 us
    pallas_call x5, Pallas kernels, kernel(): pl.pallas_call(body, out_shape=outputs[0] if single else tuple(outputs),...  4.79 us
    ppermute x1, starting transfers between devices, shards(): first1 = lax.ppermute(first1, 'chan', pairs[0])  3 us
    ppermute x3, starting transfers between devices, shards(): lax.ppermute(device, 'tm', [(i, met(i, j, parts)[0]) for i in range(parts)])  2.07 us
    ppermute x1, starting transfers between devices, shards(): second2 = lax.ppermute(second2, 'chan', pairs[1])  0.67 us
    ppermute x1, starting transfers between devices, shards(): second1 = lax.ppermute(second1, 'chan', pairs[1])  0.65 us
    ppermute x1, waiting for transfers between devices, shards(): first2 = lax.ppermute(first2, 'chan', pairs[0])  0.64 us
  transfers between devices with their start and end apart: 7, of which 1 were waited for; matrix products, arithmetic and copies ran while one was open for 0% of the time, Pallas kernels for 11%

profile of v4, /device:TPU:0, one launch (start us, length us, event | category | flops | bytes accessed | tf_op | source)
XLA Modules:
  0.0 17.6 jit_solution(17909001156631341191)
XLA Ops:
  0.0 1.5 %start.1 = (f32[16,3200]{1,0:T(8,128)S(1)}, f32[16,1408]{1,0:T(8,128)S(1)}, f32[16,1024]{1,0:T(8,128)S(1)}, f32[16,2816]{1,0:T(8,128)S(1)}, f32[32,4096]{1,0:T(8,128)S(1)}, /*index=5*/f32[32,128]{1,0:T(8,128)S(1)}) custom-call(f32[32,4096]{1,0:T(8,128)} %x_hbm.1, s32[1,32]{1,0:T(1,128)} %bitcast.1, bf16[256,256]{1,0:T(8,128)(2,1)} %constant.14.clone.gather_hbm), custom_call_target="tpu_custom_call" | custom-call | tf_op jit(solution)/shard_map/start/pallas_call | solution.py:375
  1.5 0.0 copy-start.3
  1.5 3.0 %collective-permute-start = (f32[16,3200]{1,0:T(8,128)S(1)}, f32[16,3200]{1,0:T(8,128)S(1)}, u32[]{:S(2)}, u32[]{:S(2)}) collective-permute-start(f32[16,3200]{1,0:T(8,128)S(1)} %get-tuple-element.18), channel_id=1, source_target_pairs={{0,1},{1,0},{2,3},{3,2},{4,5},{5,4},{6,7},{7,6},{8,9},{9,8},{10,11... | collective-permute-start | bytes 614408 | tf_op jit(solution)/shard_map/ppermute | solution.py:424
  4.5 0.7 %collective-permute-start.1 = (f32[16,1408]{1,0:T(8,128)S(1)}, f32[16,1408]{1,0:T(8,128)S(1)}, u32[]{:S(2)}, u32[]{:S(2)}) collective-permute-start(f32[16,1408]{1,0:T(8,128)S(1)} %get-tuple-element.19), channel_id=1, source_target_pairs={{1,2},{2,1},{3,4},{4,3},{5,6},{6,5},{9,10},{10,9},{11,12},{12,11},... | collective-permute-start | bytes 270344 | tf_op jit(solution)/shard_map/ppermute | solution.py:425
  5.2 0.7 %collective-permute-start.2 = (f32[16,2816]{1,0:T(8,128)S(1)}, f32[16,2816]{1,0:T(8,128)S(1)}, u32[]{:S(2)}, u32[]{:S(2)}) collective-permute-start(f32[16,2816]{1,0:T(8,128)S(1)} %get-tuple-element.23), channel_id=1, source_target_pairs={{1,2},{2,1},{3,4},{4,3},{5,6},{6,5},{9,10},{10,9},{11,12},{12,11},... | collective-permute-start | bytes 540680 | tf_op jit(solution)/shard_map/ppermute | solution.py:427
  5.8 5.6 %collective-permute-start.3 = (f32[16,1024]{1,0:T(8,128)S(1)}, f32[16,1024]{1,0:T(8,128)S(1)}, u32[]{:S(2)}, u32[]{:S(2)}) collective-permute-start(f32[16,1024]{1,0:T(8,128)S(1)} %get-tuple-element.25), channel_id=1, source_target_pairs={{0,1},{1,0},{2,3},{3,2},{4,5},{5,4},{6,7},{7,6},{8,9},{9,8},{10,11... | collective-permute-start | bytes 196616 | tf_op jit(solution)/shard_map/ppermute | solution.py:426
  11.4 0.0 collective-permute-done.1.second1
  11.4 0.0 collective-permute-done.first1
  11.4 0.0 copy-done.1
  11.4 0.0 copy-done.3
  11.5 0.0 copy-start
  11.5 0.0 copy-start.2
  11.5 0.3 %sums.1 = (f32[32,128]{1,0:T(8,128)S(1)}, f32[8,32]{1,0:T(8,128)S(1)}) custom-call(f32[32,128]{1,0:T(8,128)S(1)} %get-tuple-element.20.sums, f32[16,3200]{1,0:T(8,128)S(1)} %collective-permute-done.first1, f32[16,1408]{1,0:T(8,128)S(1)} %collective-permute-done.1.second1, f32[2,32,64]{2,1,0:T(8,128)S(1)} %copy-done.1, f32[8,128]{1,0:T(8,128)S(1)} %copy-done.3), custom_call_target="tpu_custom_call" | custom-call | flops 1000000000 | tf_op jit(solution)/shard_map/sums/pallas_call | solution.py:375
  11.8 0.3 %collective-permute-start.6 = (f32[8,32]{1,0:T(8,128)S(1)}, f32[8,32]{1,0:T(8,128)S(1)}, u32[]{:S(2)}, u32[]{:S(2)}) collective-permute-start(f32[8,32]{1,0:T(8,128)S(1)} %get-tuple-element.28.refs_0_), channel_id=1, source_target_pairs={{0,24},{8,16},{16,8},{24,0},{1,25},{9,17},{17,9},{25,1},{2,26},{10... | collective-permute-start | bytes 3080 | tf_op jit(solution)/shard_map/ppermute | solution.py:436
  12.1 1.7 %collective-permute-start.5 = (f32[8,32]{1,0:T(8,128)S(1)}, f32[8,32]{1,0:T(8,128)S(1)}, u32[]{:S(2)}, u32[]{:S(2)}) collective-permute-start(f32[8,32]{1,0:T(8,128)S(1)} %get-tuple-element.28.refs_0_), channel_id=1, source_target_pairs={{0,16},{8,24},{16,0},{24,8},{1,17},{9,25},{17,1},{25,9},{2,18},{10... | collective-permute-start | bytes 3080 | tf_op jit(solution)/shard_map/ppermute | solution.py:436
  13.8 0.1 collective-permute-start.4
  13.9 1.2 %early.1 = (f32[32,4096]{1,0:T(8,128)S(1)}, f32[32,128]{1,0:T(8,128)S(1)}, f32[32,128]{1,0:T(8,128)S(1)}, bf16[256,256]{1,0:T(8,128)(2,1)S(1)}) custom-call(f32[32,4096]{1,0:T(8,128)S(1)} %get-tuple-element.17.live, f32[16,3200]{1,0:T(8,128)S(1)} %collective-permute-done.first1, f32[16,1408]{1,0:T(8,128)S(1)} %collective-permute-done.1.second1, ...), custom_call_target="tpu_custom_call" | custom-call | tf_op jit(solution)/shard_map/early/pallas_call | solution.py:375
  15.1 0.0 collective-permute-done.2.second2
  15.1 0.5 %late.1.part = f32[32,4096]{1,0:T(8,128)S(1)} custom-call(f32[32,4096]{1,0:T(8,128)S(1)} %get-tuple-element.22.part, f32[16,2816]{1,0:T(8,128)S(1)} %collective-permute-done.2.second2, f32[2,32,64]{2,1,0:T(8,128)S(1)} %copy-done.1, bf16[512,256]{1,0:T(8,128)(2,1)S(1)} %copy-done), custom_call_target="tpu_custom_call" | custom-call | tf_op jit(solution)/shard_map/late/pallas_call | solution.py:375
  15.6 0.6 %collective-permute-done.3.first2 = f32[16,1024]{1,0:T(8,128)S(1)} collective-permute-done((f32[16,1024]{1,0:T(8,128)S(1)}, f32[16,1024]{1,0:T(8,128)S(1)}, u32[]{:S(2)}, u32[]{:S(2)}) %collective-permute-start.3) | collective-permute-done | bytes 65568 | tf_op jit(solution)/shard_map/ppermute | solution.py:426
  16.2 0.0 collective-permute-done.6.refs_3_
  16.2 0.0 collective-permute-done.5.refs_2_
  16.2 0.0 collective-permute-done.4.refs_1_
  16.2 1.3 %finish.1 = f32[32,4096]{1,0:T(8,128)} custom-call(f32[32,4096]{1,0:T(8,128)S(1)} %late.1.part, f32[32,128]{1,0:T(8,128)S(1)} %get-tuple-element.24.states, f32[16,1024]{1,0:T(8,128)S(1)} %collective-permute-done.3.first2, f32[2,32,64]{2,1,0:T(8,128)S(1)} %copy-done.1, bf16[512,256]{1,0:T(8,128)(2,1)S(1)} %copy-done, f32[32,128]{1,0:T(8,128)S(1)} %get-tuple-element.26.enter, ...), custom_call_target="tpu_custom_call" | custom-call | tf_op jit(solution)/shard_map/finish/pallas_call | solution.py:375
  (3 shorter events, 0.0 us)
Async XLA Ops:
  0.0 11.4 %copy-start.1 = (f32[2,32,64]{2,1,0:T(8,128)S(1)}, f32[2,32,64]{2,1,0:T(8,128)}, u32[]{:S(2)}) copy-start(f32[2,32,64]{2,1,0:T(8,128)} %constant.20.clone.mix) | copy-start | bytes 49156
  1.5 10.0 %copy-start.3 = (f32[8,128]{1,0:T(8,128)S(1)}, f32[8,128]{1,0:T(8,128)}, u32[]{:S(2)}) copy-start(f32[8,128]{1,0:T(8,128)} %constant.18.clone.whole) | copy-start | bytes 12292
  1.5 9.9 %collective-permute-start = (f32[16,3200]{1,0:T(8,128)S(1)}, f32[16,3200]{1,0:T(8,128)S(1)}, u32[]{:S(2)}, u32[]{:S(2)}) collective-permute-start(f32[16,3200]{1,0:T(8,128)S(1)} %get-tuple-element.18), channel_id=1, source_target_pairs={{0,1},{1,0},{2,3},{3,2},{4,5},{5,4},{6,7},{7,6},{8,9},{9,8},{10,11... | collective-permute-start | bytes 614408 | tf_op jit(solution)/shard_map/ppermute | solution.py:424
  4.5 6.9 %collective-permute-start.1 = (f32[16,1408]{1,0:T(8,128)S(1)}, f32[16,1408]{1,0:T(8,128)S(1)}, u32[]{:S(2)}, u32[]{:S(2)}) collective-permute-start(f32[16,1408]{1,0:T(8,128)S(1)} %get-tuple-element.19), channel_id=1, source_target_pairs={{1,2},{2,1},{3,4},{4,3},{5,6},{6,5},{9,10},{10,9},{11,12},{12,11},... | collective-permute-start | bytes 270344 | tf_op jit(solution)/shard_map/ppermute | solution.py:425
  5.2 9.9 %collective-permute-start.2 = (f32[16,2816]{1,0:T(8,128)S(1)}, f32[16,2816]{1,0:T(8,128)S(1)}, u32[]{:S(2)}, u32[]{:S(2)}) collective-permute-start(f32[16,2816]{1,0:T(8,128)S(1)} %get-tuple-element.23), channel_id=1, source_target_pairs={{1,2},{2,1},{3,4},{4,3},{5,6},{6,5},{9,10},{10,9},{11,12},{12,11},... | collective-permute-start | bytes 540680 | tf_op jit(solution)/shard_map/ppermute | solution.py:427
  5.8 10.4 %collective-permute-start.3 = (f32[16,1024]{1,0:T(8,128)S(1)}, f32[16,1024]{1,0:T(8,128)S(1)}, u32[]{:S(2)}, u32[]{:S(2)}) collective-permute-start(f32[16,1024]{1,0:T(8,128)S(1)} %get-tuple-element.25), channel_id=1, source_target_pairs={{0,1},{1,0},{2,3},{3,2},{4,5},{5,4},{6,7},{7,6},{8,9},{9,8},{10,11... | collective-permute-start | bytes 196616 | tf_op jit(solution)/shard_map/ppermute | solution.py:426
  11.5 2.4 %copy-start = (bf16[512,256]{1,0:T(8,128)(2,1)S(1)}, bf16[512,256]{1,0:T(8,128)(2,1)}, u32[]{:S(2)}) copy-start(bf16[512,256]{1,0:T(8,128)(2,1)} %constant.15.clone.toeplitz) | copy-start | bytes 786436
  11.5 2.4 %copy-start.2 = (f32[128,128]{1,0:T(8,128)S(1)}, f32[128,128]{1,0:T(8,128)}, u32[]{:S(2)}) copy-start(f32[128,128]{1,0:T(8,128)} %constant.17.clone.inner) | copy-start | bytes 196612
  11.8 4.4 %collective-permute-start.6 = (f32[8,32]{1,0:T(8,128)S(1)}, f32[8,32]{1,0:T(8,128)S(1)}, u32[]{:S(2)}, u32[]{:S(2)}) collective-permute-start(f32[8,32]{1,0:T(8,128)S(1)} %get-tuple-element.28.refs_0_), channel_id=1, source_target_pairs={{0,24},{8,16},{16,8},{24,0},{1,25},{9,17},{17,9},{25,1},{2,26},{10... | collective-permute-start | bytes 3080 | tf_op jit(solution)/shard_map/ppermute | solution.py:436
  12.1 4.2 %collective-permute-start.5 = (f32[8,32]{1,0:T(8,128)S(1)}, f32[8,32]{1,0:T(8,128)S(1)}, u32[]{:S(2)}, u32[]{:S(2)}) collective-permute-start(f32[8,32]{1,0:T(8,128)S(1)} %get-tuple-element.28.refs_0_), channel_id=1, source_target_pairs={{0,16},{8,24},{16,0},{24,8},{1,17},{9,25},{17,1},{25,9},{2,18},{10... | collective-permute-start | bytes 3080 | tf_op jit(solution)/shard_map/ppermute | solution.py:436
  13.8 2.4 %collective-permute-start.4 = (f32[8,32]{1,0:T(8,128)S(1)}, f32[8,32]{1,0:T(8,128)S(1)}, u32[]{:S(2)}, u32[]{:S(2)}) collective-permute-start(f32[8,32]{1,0:T(8,128)S(1)} %get-tuple-element.28.refs_0_), channel_id=1, source_target_pairs={{0,8},{8,0},{16,24},{24,16},{1,9},{9,1},{17,25},{25,17},{2,10},{10... | collective-permute-start | bytes 3080 | tf_op jit(solution)/shard_map/ppermute | solution.py:436

commit v5 on v4

--- a/solution.py
+++ b/solution.py
@@ -12,7 +12,7 @@
 RADIUS = 16
 BLOCK = 256
 STATES = 8
-SUMS_COST = 10
+SUMS_COST = 8
 
 low_corner = 0.015
 high_corner = 100.0
@@ -389,7 +389,7 @@
     parts = lax.axis_size("tm")
     places = lax.axis_size("chan")
     lanes = samples // BLOCK * STATES
-    cuts = (samples * 3 // 4 // BLOCK * BLOCK, samples * 5 // 16 // BLOCK * BLOCK)
+    cuts = (samples * 11 // 16 // BLOCK * BLOCK, samples * 3 // 8 // BLOCK * BLOCK)
     toeplitz, gather, spread, inner, whole, enter = time_tables(samples, parts)
     gather = jnp.asarray(np.concatenate(halves(gather), axis=1))
     toeplitz = jnp.asarray(np.concatenate(halves(toeplitz), axis=0))
@@ -450,9 +450,8 @@
         far=(7, 8),
     )
     part = kernel(late_kernel, "late", [part, second2, mix, toeplitz], [vmem(channels, samples)])
-    step = max(BLOCK, samples // 4 // BLOCK * BLOCK)
-    edges = sorted({cuts[0], samples, *range(0, samples, step)})
-    pieces = list(zip(edges[:-1], edges[1:]))[::-1]
+    middle = cuts[0] // 2 // BLOCK * BLOCK
+    pieces = [(middle, cuts[0]), (cuts[0], samples), (0, middle)]
     return kernel(
         functools.partial(finish_kernel, pieces),
         "finish",

time: 17.8 us -> 17.6 us (0.989)
  no operation moved by 1% of the time
where the time goes in v5:
time: 17.6 us; the launch traced here: 17.4 us
  starting transfers between devices  12 us (68%)
  Pallas kernels  4.65 us (26%)
  waiting for transfers between devices  0.59 us (3%)
    ppermute x1, starting transfers between devices, shards(): first2 = lax.ppermute(first2, 'chan', pairs[0])  5.59 us
    pallas_call x5, Pallas kernels, kernel(): pl.pallas_call(body, out_shape=outputs[0] if single else tuple(outputs),...  4.65 us
    ppermute x1, starting transfers between devices, shards(): first1 = lax.ppermute(first1, 'chan', pairs[0])  3 us
    ppermute x3, starting transfers between devices, shards(): lax.ppermute(device, 'tm', [(i, met(i, j, parts)[0]) for i in range(parts)])  2.07 us
    ppermute x1, starting transfers between devices, shards(): second2 = lax.ppermute(second2, 'chan', pairs[1])  0.67 us
    ppermute x1, starting transfers between devices, shards(): second1 = lax.ppermute(second1, 'chan', pairs[1])  0.66 us
    ppermute x1, waiting for transfers between devices, shards(): first2 = lax.ppermute(first2, 'chan', pairs[0])  0.57 us
  transfers between devices with their start and end apart: 7, of which 1 were waited for; matrix products, arithmetic and copies ran while one was open for 0% of the time, Pallas kernels for 11%

profile of v5, /device:TPU:0, one launch (start us, length us, event | category | flops | bytes accessed | tf_op | source)
XLA Modules:
  0.0 17.4 jit_solution(11346239334500473788)
XLA Ops:
  0.0 1.5 %start.1 = (f32[16,2944]{1,0:T(8,128)S(1)}, f32[16,1664]{1,0:T(8,128)S(1)}, f32[16,1280]{1,0:T(8,128)S(1)}, f32[16,2560]{1,0:T(8,128)S(1)}, f32[32,4096]{1,0:T(8,128)S(1)}, /*index=5*/f32[32,128]{1,0:T(8,128)S(1)}) custom-call(f32[32,4096]{1,0:T(8,128)} %x_hbm.1, s32[1,32]{1,0:T(1,128)} %bitcast.1, bf16[256,256]{1,0:T(8,128)(2,1)} %constant.14.clone.gather_hbm), custom_call_target="tpu_custom_call" | custom-call | tf_op jit(solution)/shard_map/start/pallas_call | solution.py:375
  1.5 0.0 copy-start.3
  1.5 3.0 %collective-permute-start = (f32[16,2944]{1,0:T(8,128)S(1)}, f32[16,2944]{1,0:T(8,128)S(1)}, u32[]{:S(2)}, u32[]{:S(2)}) collective-permute-start(f32[16,2944]{1,0:T(8,128)S(1)} %get-tuple-element.18), channel_id=1, source_target_pairs={{0,1},{1,0},{2,3},{3,2},{4,5},{5,4},{6,7},{7,6},{8,9},{9,8},{10,11... | collective-permute-start | bytes 565256 | tf_op jit(solution)/shard_map/ppermute | solution.py:424
  4.5 0.7 %collective-permute-start.1 = (f32[16,1664]{1,0:T(8,128)S(1)}, f32[16,1664]{1,0:T(8,128)S(1)}, u32[]{:S(2)}, u32[]{:S(2)}) collective-permute-start(f32[16,1664]{1,0:T(8,128)S(1)} %get-tuple-element.19), channel_id=1, source_target_pairs={{1,2},{2,1},{3,4},{4,3},{5,6},{6,5},{9,10},{10,9},{11,12},{12,11},... | collective-permute-start | bytes 319496 | tf_op jit(solution)/shard_map/ppermute | solution.py:425
  5.2 0.7 %collective-permute-start.2 = (f32[16,2560]{1,0:T(8,128)S(1)}, f32[16,2560]{1,0:T(8,128)S(1)}, u32[]{:S(2)}, u32[]{:S(2)}) collective-permute-start(f32[16,2560]{1,0:T(8,128)S(1)} %get-tuple-element.23), channel_id=1, source_target_pairs={{1,2},{2,1},{3,4},{4,3},{5,6},{6,5},{9,10},{10,9},{11,12},{12,11},... | collective-permute-start | bytes 491528 | tf_op jit(solution)/shard_map/ppermute | solution.py:427
  5.8 5.6 %collective-permute-start.3 = (f32[16,1280]{1,0:T(8,128)S(1)}, f32[16,1280]{1,0:T(8,128)S(1)}, u32[]{:S(2)}, u32[]{:S(2)}) collective-permute-start(f32[16,1280]{1,0:T(8,128)S(1)} %get-tuple-element.25), channel_id=1, source_target_pairs={{0,1},{1,0},{2,3},{3,2},{4,5},{5,4},{6,7},{7,6},{8,9},{9,8},{10,11... | collective-permute-start | bytes 245768 | tf_op jit(solution)/shard_map/ppermute | solution.py:426
  11.4 0.0 collective-permute-done.1.second1
  11.4 0.0 collective-permute-done.first1
  11.4 0.0 copy-done.1
  11.4 0.0 copy-done.3
  11.5 0.0 copy-start
  11.5 0.0 copy-start.2
  11.5 0.3 %sums.1 = (f32[32,128]{1,0:T(8,128)S(1)}, f32[8,32]{1,0:T(8,128)S(1)}) custom-call(f32[32,128]{1,0:T(8,128)S(1)} %get-tuple-element.20.sums, f32[16,2944]{1,0:T(8,128)S(1)} %collective-permute-done.first1, f32[16,1664]{1,0:T(8,128)S(1)} %collective-permute-done.1.second1, f32[2,32,64]{2,1,0:T(8,128)S(1)} %copy-done.1, f32[8,128]{1,0:T(8,128)S(1)} %copy-done.3), custom_call_target="tpu_custom_call" | custom-call | flops 800000000 | tf_op jit(solution)/shard_map/sums/pallas_call | solution.py:375
  11.8 0.3 %collective-permute-start.6 = (f32[8,32]{1,0:T(8,128)S(1)}, f32[8,32]{1,0:T(8,128)S(1)}, u32[]{:S(2)}, u32[]{:S(2)}) collective-permute-start(f32[8,32]{1,0:T(8,128)S(1)} %get-tuple-element.28.refs_0_), channel_id=1, source_target_pairs={{0,24},{8,16},{16,8},{24,0},{1,25},{9,17},{17,9},{25,1},{2,26},{10... | collective-permute-start | bytes 3080 | tf_op jit(solution)/shard_map/ppermute | solution.py:436
  12.1 1.7 %collective-permute-start.5 = (f32[8,32]{1,0:T(8,128)S(1)}, f32[8,32]{1,0:T(8,128)S(1)}, u32[]{:S(2)}, u32[]{:S(2)}) collective-permute-start(f32[8,32]{1,0:T(8,128)S(1)} %get-tuple-element.28.refs_0_), channel_id=1, source_target_pairs={{0,16},{8,24},{16,0},{24,8},{1,17},{9,25},{17,1},{25,9},{2,18},{10... | collective-permute-start | bytes 3080 | tf_op jit(solution)/shard_map/ppermute | solution.py:436
  13.8 0.1 collective-permute-start.4
  13.9 1.1 %early.1 = (f32[32,4096]{1,0:T(8,128)S(1)}, f32[32,128]{1,0:T(8,128)S(1)}, f32[32,128]{1,0:T(8,128)S(1)}, bf16[256,256]{1,0:T(8,128)(2,1)S(1)}) custom-call(f32[32,4096]{1,0:T(8,128)S(1)} %get-tuple-element.17.live, f32[16,2944]{1,0:T(8,128)S(1)} %collective-permute-done.first1, f32[16,1664]{1,0:T(8,128)S(1)} %collective-permute-done.1.second1, ...), custom_call_target="tpu_custom_call" | custom-call | tf_op jit(solution)/shard_map/early/pallas_call | solution.py:375
  15.0 0.0 collective-permute-done.2.second2
  15.0 0.5 %late.1.part = f32[32,4096]{1,0:T(8,128)S(1)} custom-call(f32[32,4096]{1,0:T(8,128)S(1)} %get-tuple-element.22.part, f32[16,2560]{1,0:T(8,128)S(1)} %collective-permute-done.2.second2, f32[2,32,64]{2,1,0:T(8,128)S(1)} %copy-done.1, bf16[512,256]{1,0:T(8,128)(2,1)S(1)} %copy-done), custom_call_target="tpu_custom_call" | custom-call | tf_op jit(solution)/shard_map/late/pallas_call | solution.py:375
  15.5 0.6 %collective-permute-done.3.first2 = f32[16,1280]{1,0:T(8,128)S(1)} collective-permute-done((f32[16,1280]{1,0:T(8,128)S(1)}, f32[16,1280]{1,0:T(8,128)S(1)}, u32[]{:S(2)}, u32[]{:S(2)}) %collective-permute-start.3) | collective-permute-done | bytes 81952 | tf_op jit(solution)/shard_map/ppermute | solution.py:426
  16.1 0.0 collective-permute-done.6.refs_3_
  16.1 0.0 collective-permute-done.5.refs_2_
  16.1 0.0 collective-permute-done.4.refs_1_
  16.1 1.3 %finish.1 = f32[32,4096]{1,0:T(8,128)} custom-call(f32[32,4096]{1,0:T(8,128)S(1)} %late.1.part, f32[32,128]{1,0:T(8,128)S(1)} %get-tuple-element.24.states, f32[16,1280]{1,0:T(8,128)S(1)} %collective-permute-done.3.first2, f32[2,32,64]{2,1,0:T(8,128)S(1)} %copy-done.1, bf16[512,256]{1,0:T(8,128)(2,1)S(1)} %copy-done, f32[32,128]{1,0:T(8,128)S(1)} %get-tuple-element.26.enter, ...), custom_call_target="tpu_custom_call" | custom-call | tf_op jit(solution)/shard_map/finish/pallas_call | solution.py:375
  (3 shorter events, 0.0 us)
Async XLA Ops:
  0.0 11.4 %copy-start.1 = (f32[2,32,64]{2,1,0:T(8,128)S(1)}, f32[2,32,64]{2,1,0:T(8,128)}, u32[]{:S(2)}) copy-start(f32[2,32,64]{2,1,0:T(8,128)} %constant.20.clone.mix) | copy-start | bytes 49156
  1.5 10.0 %copy-start.3 = (f32[8,128]{1,0:T(8,128)S(1)}, f32[8,128]{1,0:T(8,128)}, u32[]{:S(2)}) copy-start(f32[8,128]{1,0:T(8,128)} %constant.18.clone.whole) | copy-start | bytes 12292
  1.5 9.9 %collective-permute-start = (f32[16,2944]{1,0:T(8,128)S(1)}, f32[16,2944]{1,0:T(8,128)S(1)}, u32[]{:S(2)}, u32[]{:S(2)}) collective-permute-start(f32[16,2944]{1,0:T(8,128)S(1)} %get-tuple-element.18), channel_id=1, source_target_pairs={{0,1},{1,0},{2,3},{3,2},{4,5},{5,4},{6,7},{7,6},{8,9},{9,8},{10,11... | collective-permute-start | bytes 565256 | tf_op jit(solution)/shard_map/ppermute | solution.py:424
  4.5 6.9 %collective-permute-start.1 = (f32[16,1664]{1,0:T(8,128)S(1)}, f32[16,1664]{1,0:T(8,128)S(1)}, u32[]{:S(2)}, u32[]{:S(2)}) collective-permute-start(f32[16,1664]{1,0:T(8,128)S(1)} %get-tuple-element.19), channel_id=1, source_target_pairs={{1,2},{2,1},{3,4},{4,3},{5,6},{6,5},{9,10},{10,9},{11,12},{12,11},... | collective-permute-start | bytes 319496 | tf_op jit(solution)/shard_map/ppermute | solution.py:425
  5.2 9.9 %collective-permute-start.2 = (f32[16,2560]{1,0:T(8,128)S(1)}, f32[16,2560]{1,0:T(8,128)S(1)}, u32[]{:S(2)}, u32[]{:S(2)}) collective-permute-start(f32[16,2560]{1,0:T(8,128)S(1)} %get-tuple-element.23), channel_id=1, source_target_pairs={{1,2},{2,1},{3,4},{4,3},{5,6},{6,5},{9,10},{10,9},{11,12},{12,11},... | collective-permute-start | bytes 491528 | tf_op jit(solution)/shard_map/ppermute | solution.py:427
  5.8 10.2 %collective-permute-start.3 = (f32[16,1280]{1,0:T(8,128)S(1)}, f32[16,1280]{1,0:T(8,128)S(1)}, u32[]{:S(2)}, u32[]{:S(2)}) collective-permute-start(f32[16,1280]{1,0:T(8,128)S(1)} %get-tuple-element.25), channel_id=1, source_target_pairs={{0,1},{1,0},{2,3},{3,2},{4,5},{5,4},{6,7},{7,6},{8,9},{9,8},{10,11... | collective-permute-start | bytes 245768 | tf_op jit(solution)/shard_map/ppermute | solution.py:426
  11.5 2.4 %copy-start = (bf16[512,256]{1,0:T(8,128)(2,1)S(1)}, bf16[512,256]{1,0:T(8,128)(2,1)}, u32[]{:S(2)}) copy-start(bf16[512,256]{1,0:T(8,128)(2,1)} %constant.15.clone.toeplitz) | copy-start | bytes 786436
  11.5 2.4 %copy-start.2 = (f32[128,128]{1,0:T(8,128)S(1)}, f32[128,128]{1,0:T(8,128)}, u32[]{:S(2)}) copy-start(f32[128,128]{1,0:T(8,128)} %constant.17.clone.inner) | copy-start | bytes 196612
  11.8 4.3 %collective-permute-start.6 = (f32[8,32]{1,0:T(8,128)S(1)}, f32[8,32]{1,0:T(8,128)S(1)}, u32[]{:S(2)}, u32[]{:S(2)}) collective-permute-start(f32[8,32]{1,0:T(8,128)S(1)} %get-tuple-element.28.refs_0_), channel_id=1, source_target_pairs={{0,24},{8,16},{16,8},{24,0},{1,25},{9,17},{17,9},{25,1},{2,26},{10... | collective-permute-start | bytes 3080 | tf_op jit(solution)/shard_map/ppermute | solution.py:436
  12.1 4.0 %collective-permute-start.5 = (f32[8,32]{1,0:T(8,128)S(1)}, f32[8,32]{1,0:T(8,128)S(1)}, u32[]{:S(2)}, u32[]{:S(2)}) collective-permute-start(f32[8,32]{1,0:T(8,128)S(1)} %get-tuple-element.28.refs_0_), channel_id=1, source_target_pairs={{0,16},{8,24},{16,0},{24,8},{1,17},{9,25},{17,1},{25,9},{2,18},{10... | collective-permute-start | bytes 3080 | tf_op jit(solution)/shard_map/ppermute | solution.py:436
  13.8 2.3 %collective-permute-start.4 = (f32[8,32]{1,0:T(8,128)S(1)}, f32[8,32]{1,0:T(8,128)S(1)}, u32[]{:S(2)}, u32[]{:S(2)}) collective-permute-start(f32[8,32]{1,0:T(8,128)S(1)} %get-tuple-element.28.refs_0_), channel_id=1, source_target_pairs={{0,8},{8,0},{16,24},{24,16},{1,9},{9,1},{17,25},{25,17},{2,10},{10... | collective-permute-start | bytes 3080 | tf_op jit(solution)/shard_map/ppermute | solution.py:436

commit v6 on v5

--- a/solution.py
+++ b/solution.py
@@ -329,7 +329,6 @@
     channels, samples = part.shape
     start = samples - second2.shape[1]
     rows = edge_rows(1, second2[...], mix, toeplitz, channels)
-    out[:, :start] = part[:, :start]
     for b in range((samples - start) // BLOCK):
         here = slice(start + b * BLOCK, start + (b + 1) * BLOCK)
         out[:, here] = part[:, here] + rows[b * channels : (b + 1) * channels]
@@ -362,7 +361,7 @@
     return pltpu.VMEM(shape, dtype)
 
 
-def kernel(body, name, inputs, outputs, scratch=(), cost=0, far=()):
+def kernel(body, name, inputs, outputs, scratch=(), cost=0, far=(), aliases={}):
     inputs = [
         pltpu.with_memory_space_constraint(v, pltpu.HBM if i in far else VMEM)
         for i, v in enumerate(inputs)
@@ -380,6 +379,7 @@
         scratch_shapes=list(scratch),
         compiler_params=pltpu.CompilerParams(vmem_limit_bytes=24 * 1024 * 1024),
         cost_estimate=pl.CostEstimate(flops=cost * 100000000, bytes_accessed=0, transcendentals=0),
+        input_output_aliases=aliases,
         name=name,
     )(*inputs)
 
@@ -449,9 +449,11 @@
         [pltpu.SemaphoreType.DMA((2,))],
         far=(7, 8),
     )
-    part = kernel(late_kernel, "late", [part, second2, mix, toeplitz], [vmem(channels, samples)])
+    part = kernel(
+        late_kernel, "late", [part, second2, mix, toeplitz], [vmem(channels, samples)], aliases={0: 0}
+    )
     middle = cuts[0] // 2 // BLOCK * BLOCK
-    pieces = [(middle, cuts[0]), (cuts[0], samples), (0, middle)]
+    pieces = [(middle, cuts[0]), (cuts[0], samples), (middle // 2 // BLOCK * BLOCK, middle), (0, middle // 2 // BLOCK * BLOCK)]
     return kernel(
         functools.partial(finish_kernel, pieces),
         "finish",

time: 17.6 us -> 17.6 us (level)
  no operation moved by 1% of the time
where the time goes in v6:
time: 17.6 us; the launch traced here: 17.4 us
  starting transfers between devices  12 us (68%)
  Pallas kernels  4.67 us (27%)
  waiting for transfers between devices  0.58 us (3%)
    ppermute x1, starting transfers between devices, shards(): first2 = lax.ppermute(first2, 'chan', pairs[0])  5.59 us
    pallas_call x5, Pallas kernels, kernel(): pl.pallas_call(body, out_shape=outputs[0] if single else tuple(outputs),...  4.67 us
    ppermute x1, starting transfers between devices, shards(): first1 = lax.ppermute(first1, 'chan', pairs[0])  3 us
    ppermute x3, starting transfers between devices, shards(): lax.ppermute(device, 'tm', [(i, met(i, j, parts)[0]) for i in range(parts)])  2.07 us
    ppermute x1, starting transfers between devices, shards(): second2 = lax.ppermute(second2, 'chan', pairs[1])  0.67 us
    ppermute x1, starting transfers between devices, shards(): second1 = lax.ppermute(second1, 'chan', pairs[1])  0.66 us
    ppermute x1, waiting for transfers between devices, shards(): first2 = lax.ppermute(first2, 'chan', pairs[0])  0.56 us
  transfers between devices with their start and end apart: 7, of which 1 were waited for; matrix products, arithmetic and copies ran while one was open for 0% of the time, Pallas kernels for 11%

profile of v6, /device:TPU:0, one launch (start us, length us, event | category | flops | bytes accessed | tf_op | source)
XLA Modules:
  0.0 17.4 jit_solution(11659284026944816517)
XLA Ops:
  0.0 1.5 %start.1 = (f32[16,2944]{1,0:T(8,128)S(1)}, f32[16,1664]{1,0:T(8,128)S(1)}, f32[16,1280]{1,0:T(8,128)S(1)}, f32[16,2560]{1,0:T(8,128)S(1)}, f32[32,4096]{1,0:T(8,128)S(1)}, /*index=5*/f32[32,128]{1,0:T(8,128)S(1)}) custom-call(f32[32,4096]{1,0:T(8,128)} %x_hbm.1, s32[1,32]{1,0:T(1,128)} %bitcast.1, bf16[256,256]{1,0:T(8,128)(2,1)} %constant.14.clone.gather_hbm), custom_call_target="tpu_custom_call" | custom-call | tf_op jit(solution)/shard_map/start/pallas_call | solution.py:374
  1.5 0.0 copy-start.3
  1.5 3.0 %collective-permute-start = (f32[16,2944]{1,0:T(8,128)S(1)}, f32[16,2944]{1,0:T(8,128)S(1)}, u32[]{:S(2)}, u32[]{:S(2)}) collective-permute-start(f32[16,2944]{1,0:T(8,128)S(1)} %get-tuple-element.18), channel_id=1, source_target_pairs={{0,1},{1,0},{2,3},{3,2},{4,5},{5,4},{6,7},{7,6},{8,9},{9,8},{10,11... | collective-permute-start | bytes 565256 | tf_op jit(solution)/shard_map/ppermute | solution.py:424
  4.5 0.7 %collective-permute-start.1 = (f32[16,1664]{1,0:T(8,128)S(1)}, f32[16,1664]{1,0:T(8,128)S(1)}, u32[]{:S(2)}, u32[]{:S(2)}) collective-permute-start(f32[16,1664]{1,0:T(8,128)S(1)} %get-tuple-element.19), channel_id=1, source_target_pairs={{1,2},{2,1},{3,4},{4,3},{5,6},{6,5},{9,10},{10,9},{11,12},{12,11},... | collective-permute-start | bytes 319496 | tf_op jit(solution)/shard_map/ppermute | solution.py:425
  5.2 0.7 %collective-permute-start.2 = (f32[16,2560]{1,0:T(8,128)S(1)}, f32[16,2560]{1,0:T(8,128)S(1)}, u32[]{:S(2)}, u32[]{:S(2)}) collective-permute-start(f32[16,2560]{1,0:T(8,128)S(1)} %get-tuple-element.23), channel_id=1, source_target_pairs={{1,2},{2,1},{3,4},{4,3},{5,6},{6,5},{9,10},{10,9},{11,12},{12,11},... | collective-permute-start | bytes 491528 | tf_op jit(solution)/shard_map/ppermute | solution.py:427
  5.8 5.6 %collective-permute-start.3 = (f32[16,1280]{1,0:T(8,128)S(1)}, f32[16,1280]{1,0:T(8,128)S(1)}, u32[]{:S(2)}, u32[]{:S(2)}) collective-permute-start(f32[16,1280]{1,0:T(8,128)S(1)} %get-tuple-element.25), channel_id=1, source_target_pairs={{0,1},{1,0},{2,3},{3,2},{4,5},{5,4},{6,7},{7,6},{8,9},{9,8},{10,11... | collective-permute-start | bytes 245768 | tf_op jit(solution)/shard_map/ppermute | solution.py:426
  11.4 0.0 collective-permute-done.1.second1
  11.4 0.0 collective-permute-done.first1
  11.4 0.0 copy-done.1
  11.4 0.0 copy-done.3
  11.5 0.0 copy-start
  11.5 0.0 copy-start.2
  11.5 0.3 %sums.1 = (f32[32,128]{1,0:T(8,128)S(1)}, f32[8,32]{1,0:T(8,128)S(1)}) custom-call(f32[32,128]{1,0:T(8,128)S(1)} %get-tuple-element.20.sums, f32[16,2944]{1,0:T(8,128)S(1)} %collective-permute-done.first1, f32[16,1664]{1,0:T(8,128)S(1)} %collective-permute-done.1.second1, f32[2,32,64]{2,1,0:T(8,128)S(1)} %copy-done.1, f32[8,128]{1,0:T(8,128)S(1)} %copy-done.3), custom_call_target="tpu_custom_call" | custom-call | flops 800000000 | tf_op jit(solution)/shard_map/sums/pallas_call | solution.py:374
  11.8 0.3 %collective-permute-start.6 = (f32[8,32]{1,0:T(8,128)S(1)}, f32[8,32]{1,0:T(8,128)S(1)}, u32[]{:S(2)}, u32[]{:S(2)}) collective-permute-start(f32[8,32]{1,0:T(8,128)S(1)} %get-tuple-element.28.refs_0_), channel_id=1, source_target_pairs={{0,24},{8,16},{16,8},{24,0},{1,25},{9,17},{17,9},{25,1},{2,26},{10... | collective-permute-start | bytes 3080 | tf_op jit(solution)/shard_map/ppermute | solution.py:436
  12.1 1.7 %collective-permute-start.5 = (f32[8,32]{1,0:T(8,128)S(1)}, f32[8,32]{1,0:T(8,128)S(1)}, u32[]{:S(2)}, u32[]{:S(2)}) collective-permute-start(f32[8,32]{1,0:T(8,128)S(1)} %get-tuple-element.28.refs_0_), channel_id=1, source_target_pairs={{0,16},{8,24},{16,0},{24,8},{1,17},{9,25},{17,1},{25,9},{2,18},{10... | collective-permute-start | bytes 3080 | tf_op jit(solution)/shard_map/ppermute | solution.py:436
  13.8 0.1 collective-permute-start.4
  13.9 1.1 %early.1 = (f32[32,4096]{1,0:T(8,128)S(1)}, f32[32,128]{1,0:T(8,128)S(1)}, f32[32,128]{1,0:T(8,128)S(1)}, bf16[256,256]{1,0:T(8,128)(2,1)S(1)}) custom-call(f32[32,4096]{1,0:T(8,128)S(1)} %get-tuple-element.17.live, f32[16,2944]{1,0:T(8,128)S(1)} %collective-permute-done.first1, f32[16,1664]{1,0:T(8,128)S(1)} %collective-permute-done.1.second1, ...), custom_call_target="tpu_custom_call" | custom-call | tf_op jit(solution)/shard_map/early/pallas_call | solution.py:374
  15.0 0.0 collective-permute-done.2.second2
  15.0 0.5 %late.1.part = f32[32,4096]{1,0:T(8,128)S(1)} custom-call(f32[32,4096]{1,0:T(8,128)S(1)} %get-tuple-element.22.part, f32[16,2560]{1,0:T(8,128)S(1)} %collective-permute-done.2.second2, f32[2,32,64]{2,1,0:T(8,128)S(1)} %copy-done.1, bf16[512,256]{1,0:T(8,128)(2,1)S(1)} %copy-done), custom_call_target="tpu_custom_call", output_to_operand_aliasing={{}: (0, {})} | custom-call | tf_op jit(solution)/shard_map/late/pallas_call | solution.py:374
  15.5 0.6 %collective-permute-done.3.first2 = f32[16,1280]{1,0:T(8,128)S(1)} collective-permute-done((f32[16,1280]{1,0:T(8,128)S(1)}, f32[16,1280]{1,0:T(8,128)S(1)}, u32[]{:S(2)}, u32[]{:S(2)}) %collective-permute-start.3) | collective-permute-done | bytes 81952 | tf_op jit(solution)/shard_map/ppermute | solution.py:426
  16.1 0.0 collective-permute-done.6.refs_3_
  16.1 0.0 collective-permute-done.5.refs_2_
  16.1 0.0 collective-permute-done.4.refs_1_
  16.1 1.3 %finish.1 = f32[32,4096]{1,0:T(8,128)} custom-call(f32[32,4096]{1,0:T(8,128)S(1)} %late.1.part, f32[32,128]{1,0:T(8,128)S(1)} %get-tuple-element.24.states, f32[16,1280]{1,0:T(8,128)S(1)} %collective-permute-done.3.first2, f32[2,32,64]{2,1,0:T(8,128)S(1)} %copy-done.1, bf16[512,256]{1,0:T(8,128)(2,1)S(1)} %copy-done, f32[32,128]{1,0:T(8,128)S(1)} %get-tuple-element.26.enter, ...), custom_call_target="tpu_custom_call" | custom-call | tf_op jit(solution)/shard_map/finish/pallas_call | solution.py:374
  (3 shorter events, 0.0 us)
Async XLA Ops:
  0.0 11.4 %copy-start.1 = (f32[2,32,64]{2,1,0:T(8,128)S(1)}, f32[2,32,64]{2,1,0:T(8,128)}, u32[]{:S(2)}) copy-start(f32[2,32,64]{2,1,0:T(8,128)} %constant.20.clone.mix) | copy-start | bytes 49156
  1.5 10.0 %copy-start.3 = (f32[8,128]{1,0:T(8,128)S(1)}, f32[8,128]{1,0:T(8,128)}, u32[]{:S(2)}) copy-start(f32[8,128]{1,0:T(8,128)} %constant.18.clone.whole) | copy-start | bytes 12292
  1.5 9.9 %collective-permute-start = (f32[16,2944]{1,0:T(8,128)S(1)}, f32[16,2944]{1,0:T(8,128)S(1)}, u32[]{:S(2)}, u32[]{:S(2)}) collective-permute-start(f32[16,2944]{1,0:T(8,128)S(1)} %get-tuple-element.18), channel_id=1, source_target_pairs={{0,1},{1,0},{2,3},{3,2},{4,5},{5,4},{6,7},{7,6},{8,9},{9,8},{10,11... | collective-permute-start | bytes 565256 | tf_op jit(solution)/shard_map/ppermute | solution.py:424
  4.5 6.9 %collective-permute-start.1 = (f32[16,1664]{1,0:T(8,128)S(1)}, f32[16,1664]{1,0:T(8,128)S(1)}, u32[]{:S(2)}, u32[]{:S(2)}) collective-permute-start(f32[16,1664]{1,0:T(8,128)S(1)} %get-tuple-element.19), channel_id=1, source_target_pairs={{1,2},{2,1},{3,4},{4,3},{5,6},{6,5},{9,10},{10,9},{11,12},{12,11},... | collective-permute-start | bytes 319496 | tf_op jit(solution)/shard_map/ppermute | solution.py:425
  5.2 9.9 %collective-permute-start.2 = (f32[16,2560]{1,0:T(8,128)S(1)}, f32[16,2560]{1,0:T(8,128)S(1)}, u32[]{:S(2)}, u32[]{:S(2)}) collective-permute-start(f32[16,2560]{1,0:T(8,128)S(1)} %get-tuple-element.23), channel_id=1, source_target_pairs={{1,2},{2,1},{3,4},{4,3},{5,6},{6,5},{9,10},{10,9},{11,12},{12,11},... | collective-permute-start | bytes 491528 | tf_op jit(solution)/shard_map/ppermute | solution.py:427
  5.8 10.2 %collective-permute-start.3 = (f32[16,1280]{1,0:T(8,128)S(1)}, f32[16,1280]{1,0:T(8,128)S(1)}, u32[]{:S(2)}, u32[]{:S(2)}) collective-permute-start(f32[16,1280]{1,0:T(8,128)S(1)} %get-tuple-element.25), channel_id=1, source_target_pairs={{0,1},{1,0},{2,3},{3,2},{4,5},{5,4},{6,7},{7,6},{8,9},{9,8},{10,11... | collective-permute-start | bytes 245768 | tf_op jit(solution)/shard_map/ppermute | solution.py:426
  11.5 2.4 %copy-start = (bf16[512,256]{1,0:T(8,128)(2,1)S(1)}, bf16[512,256]{1,0:T(8,128)(2,1)}, u32[]{:S(2)}) copy-start(bf16[512,256]{1,0:T(8,128)(2,1)} %constant.15.clone.toeplitz) | copy-start | bytes 786436
  11.5 2.4 %copy-start.2 = (f32[128,128]{1,0:T(8,128)S(1)}, f32[128,128]{1,0:T(8,128)}, u32[]{:S(2)}) copy-start(f32[128,128]{1,0:T(8,128)} %constant.17.clone.inner) | copy-start | bytes 196612
  11.8 4.3 %collective-permute-start.6 = (f32[8,32]{1,0:T(8,128)S(1)}, f32[8,32]{1,0:T(8,128)S(1)}, u32[]{:S(2)}, u32[]{:S(2)}) collective-permute-start(f32[8,32]{1,0:T(8,128)S(1)} %get-tuple-element.28.refs_0_), channel_id=1, source_target_pairs={{0,24},{8,16},{16,8},{24,0},{1,25},{9,17},{17,9},{25,1},{2,26},{10... | collective-permute-start | bytes 3080 | tf_op jit(solution)/shard_map/ppermute | solution.py:436
  12.1 4.0 %collective-permute-start.5 = (f32[8,32]{1,0:T(8,128)S(1)}, f32[8,32]{1,0:T(8,128)S(1)}, u32[]{:S(2)}, u32[]{:S(2)}) collective-permute-start(f32[8,32]{1,0:T(8,128)S(1)} %get-tuple-element.28.refs_0_), channel_id=1, source_target_pairs={{0,16},{8,24},{16,0},{24,8},{1,17},{9,25},{17,1},{25,9},{2,18},{10... | collective-permute-start | bytes 3080 | tf_op jit(solution)/shard_map/ppermute | solution.py:436
  13.8 2.3 %collective-permute-start.4 = (f32[8,32]{1,0:T(8,128)S(1)}, f32[8,32]{1,0:T(8,128)S(1)}, u32[]{:S(2)}, u32[]{:S(2)}) collective-permute-start(f32[8,32]{1,0:T(8,128)S(1)} %get-tuple-element.28.refs_0_), channel_id=1, source_target_pairs={{0,8},{8,0},{16,24},{24,16},{1,9},{9,1},{17,25},{25,17},{2,10},{10... | collective-permute-start | bytes 3080 | tf_op jit(solution)/shard_map/ppermute | solution.py:436

commit v7 on v6

--- a/solution.py
+++ b/solution.py
@@ -389,7 +389,7 @@
     parts = lax.axis_size("tm")
     places = lax.axis_size("chan")
     lanes = samples // BLOCK * STATES
-    cuts = (samples * 11 // 16 // BLOCK * BLOCK, samples * 3 // 8 // BLOCK * BLOCK)
+    cuts = (samples * 11 // 16 // BLOCK * BLOCK, samples * 7 // 16 // BLOCK * BLOCK)
     toeplitz, gather, spread, inner, whole, enter = time_tables(samples, parts)
     gather = jnp.asarray(np.concatenate(halves(gather), axis=1))
     toeplitz = jnp.asarray(np.concatenate(halves(toeplitz), axis=0))

time: 17.6 us -> 17.6 us (level)
  no operation moved by 1% of the time
where the time goes in v7:
time: 17.6 us; the launch traced here: 17.3 us
  starting transfers between devices  12 us (68%)
  Pallas kernels  4.67 us (27%)
  waiting for transfers between devices  0.51 us (3%)
    ppermute x1, starting transfers between devices, shards(): first2 = lax.ppermute(first2, 'chan', pairs[0])  5.59 us
    pallas_call x5, Pallas kernels, kernel(): pl.pallas_call(body, out_shape=outputs[0] if single else tuple(outputs),...  4.67 us
    ppermute x1, starting transfers between devices, shards(): first1 = lax.ppermute(first1, 'chan', pairs[0])  3 us
    ppermute x3, starting transfers between devices, shards(): lax.ppermute(device, 'tm', [(i, met(i, j, parts)[0]) for i in range(parts)])  2.07 us
    ppermute x1, starting transfers between devices, shards(): second2 = lax.ppermute(second2, 'chan', pairs[1])  0.67 us
    ppermute x1, starting transfers between devices, shards(): second1 = lax.ppermute(second1, 'chan', pairs[1])  0.66 us
    ppermute x1, waiting for transfers between devices, shards(): first2 = lax.ppermute(first2, 'chan', pairs[0])  0.5 us
  transfers between devices with their start and end apart: 7, of which 1 were waited for; matrix products, arithmetic and copies ran while one was open for 0% of the time, Pallas kernels for 11%

profile of v7, /device:TPU:0, one launch (start us, length us, event | category | flops | bytes accessed | tf_op | source)
XLA Modules:
  0.0 17.3 jit_solution(1312536098762573910)
XLA Ops:
  0.0 1.5 %start.1 = (f32[16,2944]{1,0:T(8,128)S(1)}, f32[16,1920]{1,0:T(8,128)S(1)}, f32[16,1280]{1,0:T(8,128)S(1)}, f32[16,2304]{1,0:T(8,128)S(1)}, f32[32,4096]{1,0:T(8,128)S(1)}, /*index=5*/f32[32,128]{1,0:T(8,128)S(1)}) custom-call(f32[32,4096]{1,0:T(8,128)} %x_hbm.1, s32[1,32]{1,0:T(1,128)} %bitcast.1, bf16[256,256]{1,0:T(8,128)(2,1)} %constant.14.clone.gather_hbm), custom_call_target="tpu_custom_call" | custom-call | tf_op jit(solution)/shard_map/start/pallas_call | solution.py:374
  1.5 0.0 copy-start.3
  1.5 3.0 %collective-permute-start = (f32[16,2944]{1,0:T(8,128)S(1)}, f32[16,2944]{1,0:T(8,128)S(1)}, u32[]{:S(2)}, u32[]{:S(2)}) collective-permute-start(f32[16,2944]{1,0:T(8,128)S(1)} %get-tuple-element.18), channel_id=1, source_target_pairs={{0,1},{1,0},{2,3},{3,2},{4,5},{5,4},{6,7},{7,6},{8,9},{9,8},{10,11... | collective-permute-start | bytes 565256 | tf_op jit(solution)/shard_map/ppermute | solution.py:424
  4.5 0.7 %collective-permute-start.1 = (f32[16,1920]{1,0:T(8,128)S(1)}, f32[16,1920]{1,0:T(8,128)S(1)}, u32[]{:S(2)}, u32[]{:S(2)}) collective-permute-start(f32[16,1920]{1,0:T(8,128)S(1)} %get-tuple-element.19), channel_id=1, source_target_pairs={{1,2},{2,1},{3,4},{4,3},{5,6},{6,5},{9,10},{10,9},{11,12},{12,11},... | collective-permute-start | bytes 368648 | tf_op jit(solution)/shard_map/ppermute | solution.py:425
  5.2 0.7 %collective-permute-start.2 = (f32[16,2304]{1,0:T(8,128)S(1)}, f32[16,2304]{1,0:T(8,128)S(1)}, u32[]{:S(2)}, u32[]{:S(2)}) collective-permute-start(f32[16,2304]{1,0:T(8,128)S(1)} %get-tuple-element.23), channel_id=1, source_target_pairs={{1,2},{2,1},{3,4},{4,3},{5,6},{6,5},{9,10},{10,9},{11,12},{12,11},... | collective-permute-start | bytes 442376 | tf_op jit(solution)/shard_map/ppermute | solution.py:427
  5.8 5.6 %collective-permute-start.3 = (f32[16,1280]{1,0:T(8,128)S(1)}, f32[16,1280]{1,0:T(8,128)S(1)}, u32[]{:S(2)}, u32[]{:S(2)}) collective-permute-start(f32[16,1280]{1,0:T(8,128)S(1)} %get-tuple-element.25), channel_id=1, source_target_pairs={{0,1},{1,0},{2,3},{3,2},{4,5},{5,4},{6,7},{7,6},{8,9},{9,8},{10,11... | collective-permute-start | bytes 245768 | tf_op jit(solution)/shard_map/ppermute | solution.py:426
  11.4 0.0 collective-permute-done.1.second1
  11.4 0.0 collective-permute-done.first1
  11.4 0.0 copy-done.1
  11.4 0.0 copy-done.3
  11.5 0.0 copy-start
  11.5 0.0 copy-start.2
  11.5 0.3 %sums.1 = (f32[32,128]{1,0:T(8,128)S(1)}, f32[8,32]{1,0:T(8,128)S(1)}) custom-call(f32[32,128]{1,0:T(8,128)S(1)} %get-tuple-element.20.sums, f32[16,2944]{1,0:T(8,128)S(1)} %collective-permute-done.first1, f32[16,1920]{1,0:T(8,128)S(1)} %collective-permute-done.1.second1, f32[2,32,64]{2,1,0:T(8,128)S(1)} %copy-done.1, f32[8,128]{1,0:T(8,128)S(1)} %copy-done.3), custom_call_target="tpu_custom_call" | custom-call | flops 800000000 | tf_op jit(solution)/shard_map/sums/pallas_call | solution.py:374
  11.8 0.3 %collective-permute-start.6 = (f32[8,32]{1,0:T(8,128)S(1)}, f32[8,32]{1,0:T(8,128)S(1)}, u32[]{:S(2)}, u32[]{:S(2)}) collective-permute-start(f32[8,32]{1,0:T(8,128)S(1)} %get-tuple-element.28.refs_0_), channel_id=1, source_target_pairs={{0,24},{8,16},{16,8},{24,0},{1,25},{9,17},{17,9},{25,1},{2,26},{10... | collective-permute-start | bytes 3080 | tf_op jit(solution)/shard_map/ppermute | solution.py:436
  12.1 1.7 %collective-permute-start.5 = (f32[8,32]{1,0:T(8,128)S(1)}, f32[8,32]{1,0:T(8,128)S(1)}, u32[]{:S(2)}, u32[]{:S(2)}) collective-permute-start(f32[8,32]{1,0:T(8,128)S(1)} %get-tuple-element.28.refs_0_), channel_id=1, source_target_pairs={{0,16},{8,24},{16,0},{24,8},{1,17},{9,25},{17,1},{25,9},{2,18},{10... | collective-permute-start | bytes 3080 | tf_op jit(solution)/shard_map/ppermute | solution.py:436
  13.8 0.1 collective-permute-start.4
  13.9 1.1 %early.1 = (f32[32,4096]{1,0:T(8,128)S(1)}, f32[32,128]{1,0:T(8,128)S(1)}, f32[32,128]{1,0:T(8,128)S(1)}, bf16[256,256]{1,0:T(8,128)(2,1)S(1)}) custom-call(f32[32,4096]{1,0:T(8,128)S(1)} %get-tuple-element.17.live, f32[16,2944]{1,0:T(8,128)S(1)} %collective-permute-done.first1, f32[16,1920]{1,0:T(8,128)S(1)} %collective-permute-done.1.second1, ...), custom_call_target="tpu_custom_call" | custom-call | tf_op jit(solution)/shard_map/early/pallas_call | solution.py:374
  15.0 0.0 collective-permute-done.2.second2
  15.0 0.5 %late.1.part = f32[32,4096]{1,0:T(8,128)S(1)} custom-call(f32[32,4096]{1,0:T(8,128)S(1)} %get-tuple-element.22.part, f32[16,2304]{1,0:T(8,128)S(1)} %collective-permute-done.2.second2, f32[2,32,64]{2,1,0:T(8,128)S(1)} %copy-done.1, bf16[512,256]{1,0:T(8,128)(2,1)S(1)} %copy-done), custom_call_target="tpu_custom_call", output_to_operand_aliasing={{}: (0, {})} | custom-call | tf_op jit(solution)/shard_map/late/pallas_call | solution.py:374
  15.5 0.5 %collective-permute-done.3.first2 = f32[16,1280]{1,0:T(8,128)S(1)} collective-permute-done((f32[16,1280]{1,0:T(8,128)S(1)}, f32[16,1280]{1,0:T(8,128)S(1)}, u32[]{:S(2)}, u32[]{:S(2)}) %collective-permute-start.3) | collective-permute-done | bytes 81952 | tf_op jit(solution)/shard_map/ppermute | solution.py:426
  16.0 0.0 collective-permute-done.6.refs_3_
  16.0 0.0 collective-permute-done.5.refs_2_
  16.0 0.0 collective-permute-done.4.refs_1_
  16.0 1.3 %finish.1 = f32[32,4096]{1,0:T(8,128)} custom-call(f32[32,4096]{1,0:T(8,128)S(1)} %late.1.part, f32[32,128]{1,0:T(8,128)S(1)} %get-tuple-element.24.states, f32[16,1280]{1,0:T(8,128)S(1)} %collective-permute-done.3.first2, f32[2,32,64]{2,1,0:T(8,128)S(1)} %copy-done.1, bf16[512,256]{1,0:T(8,128)(2,1)S(1)} %copy-done, f32[32,128]{1,0:T(8,128)S(1)} %get-tuple-element.26.enter, ...), custom_call_target="tpu_custom_call" | custom-call | tf_op jit(solution)/shard_map/finish/pallas_call | solution.py:374
  (3 shorter events, 0.0 us)
Async XLA Ops:
  0.0 11.4 %copy-start.1 = (f32[2,32,64]{2,1,0:T(8,128)S(1)}, f32[2,32,64]{2,1,0:T(8,128)}, u32[]{:S(2)}) copy-start(f32[2,32,64]{2,1,0:T(8,128)} %constant.20.clone.mix) | copy-start | bytes 49156
  1.5 10.0 %copy-start.3 = (f32[8,128]{1,0:T(8,128)S(1)}, f32[8,128]{1,0:T(8,128)}, u32[]{:S(2)}) copy-start(f32[8,128]{1,0:T(8,128)} %constant.18.clone.whole) | copy-start | bytes 12292
  1.5 9.9 %collective-permute-start = (f32[16,2944]{1,0:T(8,128)S(1)}, f32[16,2944]{1,0:T(8,128)S(1)}, u32[]{:S(2)}, u32[]{:S(2)}) collective-permute-start(f32[16,2944]{1,0:T(8,128)S(1)} %get-tuple-element.18), channel_id=1, source_target_pairs={{0,1},{1,0},{2,3},{3,2},{4,5},{5,4},{6,7},{7,6},{8,9},{9,8},{10,11... | collective-permute-start | bytes 565256 | tf_op jit(solution)/shard_map/ppermute | solution.py:424
  4.5 6.9 %collective-permute-start.1 = (f32[16,1920]{1,0:T(8,128)S(1)}, f32[16,1920]{1,0:T(8,128)S(1)}, u32[]{:S(2)}, u32[]{:S(2)}) collective-permute-start(f32[16,1920]{1,0:T(8,128)S(1)} %get-tuple-element.19), channel_id=1, source_target_pairs={{1,2},{2,1},{3,4},{4,3},{5,6},{6,5},{9,10},{10,9},{11,12},{12,11},... | collective-permute-start | bytes 368648 | tf_op jit(solution)/shard_map/ppermute | solution.py:425
  5.2 9.9 %collective-permute-start.2 = (f32[16,2304]{1,0:T(8,128)S(1)}, f32[16,2304]{1,0:T(8,128)S(1)}, u32[]{:S(2)}, u32[]{:S(2)}) collective-permute-start(f32[16,2304]{1,0:T(8,128)S(1)} %get-tuple-element.23), channel_id=1, source_target_pairs={{1,2},{2,1},{3,4},{4,3},{5,6},{6,5},{9,10},{10,9},{11,12},{12,11},... | collective-permute-start | bytes 442376 | tf_op jit(solution)/shard_map/ppermute | solution.py:427
  5.8 10.2 %collective-permute-start.3 = (f32[16,1280]{1,0:T(8,128)S(1)}, f32[16,1280]{1,0:T(8,128)S(1)}, u32[]{:S(2)}, u32[]{:S(2)}) collective-permute-start(f32[16,1280]{1,0:T(8,128)S(1)} %get-tuple-element.25), channel_id=1, source_target_pairs={{0,1},{1,0},{2,3},{3,2},{4,5},{5,4},{6,7},{7,6},{8,9},{9,8},{10,11... | collective-permute-start | bytes 245768 | tf_op jit(solution)/shard_map/ppermute | solution.py:426
  11.5 2.4 %copy-start = (bf16[512,256]{1,0:T(8,128)(2,1)S(1)}, bf16[512,256]{1,0:T(8,128)(2,1)}, u32[]{:S(2)}) copy-start(bf16[512,256]{1,0:T(8,128)(2,1)} %constant.15.clone.toeplitz) | copy-start | bytes 786436
  11.5 2.4 %copy-start.2 = (f32[128,128]{1,0:T(8,128)S(1)}, f32[128,128]{1,0:T(8,128)}, u32[]{:S(2)}) copy-start(f32[128,128]{1,0:T(8,128)} %constant.17.clone.inner) | copy-start | bytes 196612
  11.8 4.2 %collective-permute-start.6 = (f32[8,32]{1,0:T(8,128)S(1)}, f32[8,32]{1,0:T(8,128)S(1)}, u32[]{:S(2)}, u32[]{:S(2)}) collective-permute-start(f32[8,32]{1,0:T(8,128)S(1)} %get-tuple-element.28.refs_0_), channel_id=1, source_target_pairs={{0,24},{8,16},{16,8},{24,0},{1,25},{9,17},{17,9},{25,1},{2,26},{10... | collective-permute-start | bytes 3080 | tf_op jit(solution)/shard_map/ppermute | solution.py:436
  12.1 4.0 %collective-permute-start.5 = (f32[8,32]{1,0:T(8,128)S(1)}, f32[8,32]{1,0:T(8,128)S(1)}, u32[]{:S(2)}, u32[]{:S(2)}) collective-permute-start(f32[8,32]{1,0:T(8,128)S(1)} %get-tuple-element.28.refs_0_), channel_id=1, source_target_pairs={{0,16},{8,24},{16,0},{24,8},{1,17},{9,25},{17,1},{25,9},{2,18},{10... | collective-permute-start | bytes 3080 | tf_op jit(solution)/shard_map/ppermute | solution.py:436
  13.8 2.3 %collective-permute-start.4 = (f32[8,32]{1,0:T(8,128)S(1)}, f32[8,32]{1,0:T(8,128)S(1)}, u32[]{:S(2)}, u32[]{:S(2)}) collective-permute-start(f32[8,32]{1,0:T(8,128)S(1)} %get-tuple-element.28.refs_0_), channel_id=1, source_target_pairs={{0,8},{8,0},{16,24},{24,16},{1,9},{9,1},{17,25},{25,17},{2,10},{10... | collective-permute-start | bytes 3080 | tf_op jit(solution)/shard_map/ppermute | solution.py:436
